TPU v7x, 128 devices: a whole 4x4x4 slice. The times are simulated.
128 devices in a mesh: band: 8 (over z, core), sector: 16 (over y, x).
Axes of the slice: x: 4, y: 4, z: 4, core: 2. Of those that a mesh axis runs over, the one named last changes fastest.
Arguments:
- field: float32 [2, 640, 2, 2560], P(None, 'band', None, 'sector'), may hold values from -6 to 6
- depart: int32 [2, 640, 80], P(None, 'band', 'sector'), may hold values from -2 to 2
- interp_weight: bfloat16 [2, 640, 80, 64, 32], P(None, 'band', 'sector'), may hold values from -0.75 to 0.75
- legendre: float32 [640, 640, 1281], P('sector', 'band'), may hold values from -0.25 to 0.25
- damping: float32 [2], replicated, may hold values from 0.3 to 30
Outputs:
- new_field: float32 [2, 640, 2, 2560], P(None, 'band', None, 'sector')
All inputs are finite; a program needn't handle non-finite values.
Results may differ from a plain program's by a relative error of at most 0.0003.
Values sent between devices are 32-bit elements; how exact they have to be, the bound alone decides.
A program may use at most 192 MiB of HBM per device.

v0:
```python
import math

import jax
import jax.numpy as jnp
from jax import lax
from jax.sharding import Mesh
from jax.sharding import PartitionSpec as P

SECTOR = ("sector_0", "sector_1")


HIGHEST = lax.Precision.HIGHEST


def padded(x, sides, width):
    for axis, dim in sides:
        peers, length = (lax.axis_size(axis), x.shape[dim])
        up = [(i, (i + 1) % peers) for i in range(peers)]
        down = [(j, i) for i, j in up]
        last = lax.slice_in_dim(x, length - width, length, axis=dim)
        leading = lax.slice_in_dim(x, 0, width, axis=dim)
        before = lax.ppermute(last, axis, up)
        after = lax.ppermute(leading, axis, down)
        x = jnp.concatenate([before, x, after], axis=dim)
    return x


def split_up(x, dim, peers):
    before, after = (x.shape[:dim], x.shape[dim + 1 :])
    return jnp.moveaxis(x.reshape(*before, peers, -1, *after), dim, 0)


def joined_along(pieces, dim):
    pieces = jnp.moveaxis(pieces, 0, dim)
    lengths = pieces.shape
    return pieces.reshape(*lengths[:dim], lengths[dim] * lengths[dim + 1], *lengths[dim + 2 :])


def moved_by_axis(pieces, axes, sequence):
    lengths = [lax.axis_size(a) for a in axes]
    pieces = pieces.reshape(*lengths, *pieces.shape[1:])
    for k in sequence:
        pieces = lax.all_to_all(pieces, axes[k], split_axis=k, concat_axis=k, tiled=True)
    return pieces.reshape(-1, *pieces.shape[len(axes) :])


def one_axis_at_a_time(x, axes, sequence, split_dim, concat_dim):
    pieces = split_up(x, split_dim, lax.axis_size(axes))
    return joined_along(moved_by_axis(pieces, axes, sequence), concat_dim)


def summed_on_arrival(x, axis, dim):
    peers = lax.axis_size(axis)
    pieces = lax.all_to_all(split_up(x, dim, peers), axis, 0, 0, tiled=True)
    return jnp.sum(pieces, axis=0)


def from_everyone(x, axis):
    copies = jnp.broadcast_to(x, (lax.axis_size(axis), *x.shape))
    return lax.all_to_all(copies, axis, split_axis=0, concat_axis=0, tiled=True)


def gathered_copies(x, axis, dim):
    return joined_along(from_everyone(x, axis), dim)


def phase(product, lon_count):
    return 2.0 * math.pi / lon_count * (product % lon_count).astype(jnp.float32)


def forward_table(lon_count, m_count, pair_total):
    longitude = jnp.arange(lon_count, dtype=jnp.int32)[:, None]
    pair_range = jnp.arange(pair_total, dtype=jnp.int32)[None, :]
    lower_angle = phase(longitude * pair_range, lon_count)
    upper_angle = phase(longitude * (m_count - 1 - pair_range), lon_count)
    table = jnp.stack(
        [jnp.cos(lower_angle), -jnp.sin(lower_angle), jnp.cos(upper_angle), -jnp.sin(upper_angle)],
        axis=1,
    )
    return table / lon_count


def inverse_table(lon_count, m_count, pair_total):
    pair_range = jnp.arange(pair_total, dtype=jnp.int32)[:, None]
    longitude = jnp.arange(lon_count, dtype=jnp.int32)[None, :]
    lower_angle = phase(pair_range * longitude, lon_count)
    upper_angle = phase((m_count - 1 - pair_range) * longitude, lon_count)
    lower_scale = jnp.where(pair_range == 0, 1.0, 2.0)
    return jnp.stack(
        [
            lower_scale * jnp.cos(lower_angle),
            -lower_scale * jnp.sin(lower_angle),
            2.0 * jnp.cos(upper_angle),
            -2.0 * jnp.sin(upper_angle),
        ],
        axis=0,
    )


def pair_masks(pair_index, m_count, row_count):
    column = jnp.arange(row_count, dtype=jnp.int32)[None, :]
    limit = (m_count - pair_index)[:, None]
    leading = column < limit
    lag_value = jnp.where(leading, column, column - limit)
    odd_rows = lag_value % 2 == 1
    degree = jnp.where(leading, pair_index[:, None] + column, column - 1)
    return (leading, odd_rows, degree)


def analyse(wave, legendre, leading, odd_rows):
    stacked = jnp.stack([wave[0] + wave[1], wave[0] - wave[1]])
    product = jnp.einsum("svcpl,plk->svcpk", stacked, legendre, precision=HIGHEST)
    chosen = jnp.where(odd_rows, product[1], product[0])
    return jnp.where(leading, chosen[:, 0:2], chosen[:, 2:4])


def solve_modes(spectrum, damping_levels, degree, m_count):
    ratio = (degree * (degree + 1)).astype(jnp.float32) / float(m_count * m_count)
    return spectrum / (1.0 + damping_levels[:, None, None, None] * ratio[None, None])


def synthesise(spectrum, legendre, leading, odd_rows):
    lower = jnp.where(leading, spectrum, 0.0)
    upper = jnp.where(leading, 0.0, spectrum)
    northern = jnp.concatenate([lower, upper], axis=1)
    southern = jnp.where(odd_rows, -northern, northern)
    stacked = jnp.stack([northern, southern])
    return jnp.einsum("hvcpk,plk->hvcpl", stacked, legendre, precision=HIGHEST)


def advect(field, depart, interp_weight):
    tile_width = interp_weight.shape[-1]
    tile_count = depart.shape[2]
    extended = padded(field, ((SECTOR, 3),), 3 * tile_width)
    pieces = extended.reshape(
        field.shape[0], field.shape[1], field.shape[2], tile_count + 6, tile_width
    )
    window = jnp.zeros(field.shape[:3] + (tile_count, 2 * tile_width), jnp.float32)
    for offset in range(-2, 3):
        lead_part = pieces[:, :, :, 3 + offset : 3 + offset + tile_count]
        next_part = pieces[:, :, :, 4 + offset : 4 + offset + tile_count]
        candidate = jnp.concatenate([lead_part, next_part], axis=4)
        window = jnp.where((depart == offset)[:, :, None, :, None], candidate, window)
    result = jnp.einsum(
        "hlvtj,hltji->hlvti", window, interp_weight.astype(jnp.float32), precision=HIGHEST
    )
    return result.reshape(field.shape)


def local(field, depart, interp_weight, legendre, damping):
    advected = advect(field, depart, interp_weight)
    columns = lax.all_to_all(advected, SECTOR, split_axis=1, concat_axis=3, tiled=True)
    lon_count = columns.shape[3]
    row_count = legendre.shape[2]
    m_count = row_count - 1
    pair_total = m_count // 2
    fourier = jnp.einsum(
        "hlvn,ncp->hvcpl", columns, forward_table(lon_count, m_count, pair_total), precision=HIGHEST
    )
    wave = one_axis_at_a_time(fourier, SECTOR, (0, 1), 3, 4)
    pair_local = legendre.shape[0]
    pair_index = lax.axis_index(SECTOR) * pair_local + jnp.arange(pair_local, dtype=jnp.int32)
    leading, odd_rows, degree = pair_masks(pair_index, m_count, row_count)
    partial_value = analyse(wave, legendre, leading, odd_rows)
    summed = summed_on_arrival(partial_value, "band", 2)
    pair_share = summed.shape[2]
    local_degree = lax.dynamic_slice_in_dim(
        degree, lax.axis_index("band") * pair_share, pair_share, 0
    )
    solved = solve_modes(summed, damping, local_degree, m_count)
    spectrum = gathered_copies(solved, "band", 2)
    synthesis = synthesise(spectrum, legendre, leading, odd_rows)
    returned = lax.all_to_all(synthesis, SECTOR, split_axis=4, concat_axis=3, tiled=True)
    gridded = jnp.einsum(
        "hvcpl,cpn->hlvn",
        returned,
        inverse_table(lon_count, m_count, pair_total),
        precision=HIGHEST,
    )
    return lax.all_to_all(gridded, SECTOR, split_axis=3, concat_axis=1, tiled=True)


def solution(mesh):
    finer = Mesh(mesh.devices.reshape(mesh.shape["band"], 4, 4), ("band", "sector_0", "sector_1"))
    placed = (
        P(None, "band", None, SECTOR),
        P(None, "band", SECTOR),
        P(None, "band", SECTOR, None, None),
        P(SECTOR, "band", None),
        P(),
    )
    return jax.shard_map(
        local, mesh=finer, in_specs=placed, out_specs=P(None, "band", None, SECTOR), check_vma=False
    )
```

profile of v0, /device:TPU:0, one launch (start us, length us, event | category | flops | bytes accessed | tf_op | source)
XLA Modules:
  0.0 337.9 jit_solution(17190012963628961366)
XLA Ops:
  1.2 1.6 collective-permute-start
  2.8 3.8 %collective-permute-start.1 = (f32[2,80,2,96]{1,3,2,0:T(8,128)S(1)}, f32[2,80,2,96]{1,3,2,0:T(8,128)S(1)}, u32[]{:S(2)}, u32[]{:S(2)}) collective-permute-start(f32[2,80,2,96]{1,3,2,0:T(8,128)S(1)} %get-tuple-element.16), channel_id=1, source_target_pairs={{1,0},{2,1},{3,2},{4,3},{5,4},{6,5},{7,6},{8,7},{9,8},{10,9},{11,1... | collective-permute-start | bytes 368648 | tf_op jit(solution)/shard_map/ppermute | solution.py:23
  6.6 28.3 %fusion.31 = (f32[2560,1,640]{2,0,1:T(8,128)}, f32[2560,1,640]{2,0,1:T(8,128)}) fusion(s32[640]{0:T(1024)S(1)} %iota_subtract_fusion), kind=kLoop, calls=%fused_computation.38 | loop fusion | flops 16384000 | bytes 13109760 | tf_op jit(solution)/shard_map/cos | solution.py:77
  35.1 9.4 %copy.142 = bf16[2,80,5,64,32]{3,4,2,1,0:T(8,128)(2,1)} copy(bf16[2,80,5,64,32]{1,4,3,2,0:T(8,128)(2,1)} %param.7) | data formatting | bytes 6553600 | tf_op args[2]
  45.9 12.3 %convolution_bitcast_fusion = f32[2,80,2,5,32]{4,2,3,1,0:T(2,128)S(1)} fusion(f32[2,80,2,5,64]{4,2,3,1,0:T(2,128)S(1)} %copy.141, bf16[2,80,5,64,32]{3,4,2,1,0:T(8,128)(2,1)} %copy.142), kind=kOutput, calls=%fused_computation.67 | convolution fusion | flops 39321600 | bytes 3891200 | tf_op jit(solution)/shard_map/hlvtj,hltji->hlvti/dot_general | solution.py:144
  59.5 4.3 %all-to-all-start = ((f32[2,80,2,160]{3,2,0,1:T(2,128)}), f32[2,80,2,160]{3,2,0,1:T(2,128)S(1)}, u32[]{:S(2)}, u32[]{:S(2)}) async-start(f32[2,80,2,160]{3,2,0,1:T(2,128)} %copy.144), calls=%async_computation | async-start | bytes 655360 | tf_op jit(solution)/shard_map/all_to_all | solution.py:152
  63.8 27.9 %sine_negate_fusion.1 = (f32[2560,1,640]{2,0,1:T(8,128)}, f32[2560,1,640]{2,0,1:T(8,128)}) fusion(), kind=kLoop, calls=%fused_computation.39 | loop fusion | flops 16384000 | bytes 13107200 | tf_op jit(solution)/shard_map/neg | solution.py:77
  92.0 19.0 %fusion.54 = f32[2,2,4,640,5]{3,4,1,0,2:T(8,128)S(1)} fusion(f32[2,5,2,2560,1]{3,1,2,0,4:T(8,128)S(1)} %reshape.487, f32[2560,1,640]{2,0,1:T(8,128)} %get-tuple-element.25, f32[2560,1,640]{2,0,1:T(8,128)} %get-tuple-element.24, f32[2560,1,640]{2,0,1:T(8,128)} %get-tuple-element.28, f32[2560,1,640]{2,0,1:T(8,128)} %get-tuple-element.29), kind=kOutput, calls=%fused_computation.69 | convolution fusion | flops 1599078400 | bytes 26624000 | tf_op jit(solution)/shard_map/hlvn,ncp->hvcpl/dot_general | solution.py:157
  111.8 1.6 reshape.494
  113.4 4.8 %all-to-all-start.1 = ((f32[4,1,12800]{2,1,0:T(1,128)}), f32[4,1,12800]{2,1,0:T(1,128)S(1)}, u32[]{:S(2)}, u32[]{:S(2)}) async-start(f32[4,1,12800]{2,1,0:T(1,128)} %reshape.494), calls=%async_computation.1 | async-start | bytes 409600 | tf_op jit(solution)/shard_map/all_to_all | solution.py:43
  118.2 6.4 %all-to-all-done.1 = f32[4,1,12800]{2,1,0:T(1,128)S(1)} async-done(((f32[4,1,12800]{2,1,0:T(1,128)}), f32[4,1,12800]{2,1,0:T(1,128)S(1)}, u32[]{:S(2)}, u32[]{:S(2)}) %all-to-all-start.1) | async-done | bytes 204832 | tf_op jit(solution)/shard_map/all_to_all | solution.py:43
  125.1 1.2 reduce
  127.8 1.6 reshape.496
  129.4 4.4 %all-to-all-start.2 = ((f32[4,1,12800]{2,1,0:T(1,128)}), f32[4,1,12800]{2,1,0:T(1,128)S(1)}, u32[]{:S(2)}, u32[]{:S(2)}) async-start(f32[4,1,12800]{2,1,0:T(1,128)} %reshape.496), calls=%async_computation.2 | async-start | bytes 409600 | tf_op jit(solution)/shard_map/all_to_all | solution.py:43
  134.1 6.0 %all-to-all-done.2 = f32[4,1,12800]{2,1,0:T(1,128)S(1)} async-done(((f32[4,1,12800]{2,1,0:T(1,128)}), f32[4,1,12800]{2,1,0:T(1,128)S(1)}, u32[]{:S(2)}, u32[]{:S(2)}) %all-to-all-start.2) | async-done | bytes 204832 | tf_op jit(solution)/shard_map/all_to_all | solution.py:43
  140.1 1.2 reduce.1
  143.4 12.7 %fusion.44 = f32[2,2,4,40,1281]{4,2,1,0,3:T(4,128)S(1)} fusion(f32[40,80,1281]{2,1,0:T(8,128)} %param.8, f32[1,2,4,40,80]{4,2,1,0,3:T(4,128)S(1)} %copy.155, f32[1,2,4,40,80]{4,2,1,0,3:T(4,128)S(1)} %copy.154), kind=kOutput, calls=%fused_computation.60 | convolution fusion | flops 787097600 | bytes 19880960 | tf_op jit(solution)/shard_map/svcpl,plk->svcpk/dot_general | solution.py:112
  156.7 1.6 slice_select_fusion
  158.3 5.3 %all-to-all-start.3 = ((f32[8,2,2,5,1281]{4,2,1,3,0:T(2,128)}), f32[8,2,2,5,1281]{4,2,1,3,0:T(2,128)S(1)}, u32[]{:S(2)}, u32[]{:S(2)}) async-start(f32[8,2,2,5,1281]{4,2,1,3,0:T(2,128)} %bitcast.24), calls=%async_computation.3 | async-start | bytes 1802240 | tf_op jit(solution)/shard_map/all_to_all | solution.py:54
  163.8 14.2 %all-to-all-done.3 = f32[8,2,2,5,1281]{4,2,1,3,0:T(2,128)S(1)} async-done(((f32[8,2,2,5,1281]{4,2,1,3,0:T(2,128)}), f32[8,2,2,5,1281]{4,2,1,3,0:T(2,128)S(1)}, u32[]{:S(2)}, u32[]{:S(2)}) %all-to-all-start.3) | async-done | bytes 819872 | tf_op jit(solution)/shard_map/all_to_all | solution.py:54
  179.6 3.8 %all-to-all-start.4 = ((f32[8,2,2,5,1281]{4,2,1,3,0:T(2,128)}), f32[8,2,2,5,1281]{4,2,1,3,0:T(2,128)S(1)}, u32[]{:S(2)}, u32[]{:S(2)}) async-start(f32[8,2,2,5,1281]{4,2,1,3,0:T(2,128)} %broadcast_in_dim.102), calls=%async_computation.4 | async-start | bytes 1802240 | tf_op jit(solution)/shard_map/all_to_all | solution.py:60
  183.4 28.3 %sine_multiply_fusion.1 = (f32[1,640,2560]{2,1,0:T(8,128)}, f32[1,640,2560]{2,1,0:T(8,128)}) fusion(f32[640]{0:T(1024)S(1)} %fusion.66, f32[640]{0:T(1024)S(1)} %fusion.65), kind=kLoop, calls=%fused_computation.49 | loop fusion | flops 18022400 | bytes 13112320 | tf_op jit(solution)/shard_map/mul | solution.py:92
  214.5 20.8 %fusion.49 = f32[2,2,4,40,80]{4,2,1,0,3:T(4,128)S(1)} fusion(f32[40,80,1281]{2,1,0:T(8,128)} %param.8, f32[1,2,4,40,1281]{4,2,1,3,0:T(4,128)S(1)} %negate_select_fusion, f32[1,2,4,40,1281]{4,2,1,3,0:T(4,128)S(1)} %maximum_bitcast_fusion.4), kind=kOutput, calls=%fused_computation.68 | convolution fusion | flops 787866240 | bytes 19880960 | tf_op jit(solution)/shard_map/hvcpk,plk->hvcpl/dot_general | solution.py:128
  235.8 1.6 reshape.498
  237.4 3.8 %all-to-all-start.5 = ((f32[16,1,3200]{2,1,0:T(1,128)}), f32[16,1,3200]{2,1,0:T(1,128)S(1)}, u32[]{:S(2)}, u32[]{:S(2)}) async-start(f32[16,1,3200]{2,1,0:T(1,128)} %reshape.498), calls=%async_computation.5 | async-start | bytes 409600 | tf_op jit(solution)/shard_map/all_to_all | solution.py:173
  241.2 29.7 %cosine_multiply_fusion = (f32[1,640,2560]{2,1,0:T(8,128)}, f32[1,640,2560]{2,1,0:T(8,128)}) fusion(s32[640]{0:T(1024)S(1)} %iota_subtract_fusion), kind=kLoop, calls=%fused_computation.45 | loop fusion | flops 18022400 | bytes 13109760 | tf_op jit(solution)/shard_map/mul | solution.py:93
  273.6 17.7 %fusion.47 = f32[2,5,2,2560]{3,1,2,0:T(8,128)S(1)} fusion(f32[2,2,4,640,5]{3,4,2,1,0:T(8,128)S(1)} %reshape.493, f32[1,640,2560]{2,1,0:T(8,128)} %get-tuple-element.23, f32[1,640,2560]{2,1,0:T(8,128)} %get-tuple-element.22, f32[1,640,2560]{2,1,0:T(8,128)} %get-tuple-element.32, f32[1,640,2560]{2,1,0:T(8,128)} %get-tuple-element.33), kind=kOutput, calls=%fused_computation.61 | convolution fusion | flops 1592524800 | bytes 26624000 | tf_op jit(solution)/shard_map/hvcpl,cpn->hlvn/dot_general | solution.py:174
  291.4 4.9 %copy.162 = f32[2,5,2,2560]{1,2,0,3:T(2,128)} copy(f32[2,5,2,2560]{3,1,2,0:T(8,128)S(1)} %fusion.47) | data formatting | bytes 409600 | tf_op jit(solution)/shard_map/hvcpl,cpn->hlvn/transpose | solution.py:174
  296.3 7.2 %reshape.500 = f32[16,1,3200]{2,1,0:T(1,128)S(1)} reshape(f32[2560,2,2,5]{3,2,1,0:T(2,128)} %bitcast.105) | data formatting | bytes 409600
  303.5 15.7 %all_to_all.74 = f32[16,1,3200]{2,1,0:T(1,128)S(1)} all-to-all(f32[16,1,3200]{2,1,0:T(1,128)S(1)} %reshape.500), channel_id=1, replica_groups=mesh['band'=8,'sector_0'=4,'sector_1'=4] {'sector_0','sector_1'}, dimensions={0} | all-to-all | bytes 409600 | tf_op jit(solution)/shard_map/all_to_all | solution.py:180
  320.4 9.4 %reshape.501 = f32[2560,2,2,5]{3,2,1,0:T(2,128)} reshape(f32[16,3200]{1,0:T(8,128)S(1)} %reduce.3) | data formatting | bytes 409600
  329.8 6.6 %copy.173 = f32[2,5,2,16,160]{4,3,2,1,0:T(8,128)S(1)} copy(f32[2,5,2,16,160]{1,2,0,4,3:T(2,128)} %bitcast.106) | data formatting | bytes 409600 | tf_op jit(solution)/shard_map/all_to_all | solution.py:180
  (61 shorter events, 19.8 us)
Async XLA Ops:
  1.2 43.3 %collective-permute-start = (f32[2,80,2,96]{1,3,2,0:T(8,128)S(1)}, f32[2,80,2,96]{1,3,2,0:T(8,128)S(1)}, u32[]{:S(2)}, u32[]{:S(2)}) collective-permute-start(f32[2,80,2,96]{1,3,2,0:T(8,128)S(1)} %get-tuple-element.15), channel_id=1, source_target_pairs={{0,1},{1,2},{2,3},{3,4},{4,5},{5,6},{6,7},{7,8},{8,9},{9,10},{10,1... | collective-permute-start | bytes 368648 | tf_op jit(solution)/shard_map/ppermute | solution.py:22
  2.8 41.7 %collective-permute-start.1 = (f32[2,80,2,96]{1,3,2,0:T(8,128)S(1)}, f32[2,80,2,96]{1,3,2,0:T(8,128)S(1)}, u32[]{:S(2)}, u32[]{:S(2)}) collective-permute-start(f32[2,80,2,96]{1,3,2,0:T(8,128)S(1)} %get-tuple-element.16), channel_id=1, source_target_pairs={{1,0},{2,1},{3,2},{4,3},{5,4},{6,5},{7,6},{8,7},{9,8},{10,9},{11,1... | collective-permute-start | bytes 368648 | tf_op jit(solution)/shard_map/ppermute | solution.py:23
  6.6 28.4 %copy-start = (s32[2,80,5]{1,0,2:T(2,128)S(1)}, s32[2,80,5]{1,0,2:T(2,128)}, u32[]{:S(2)}) copy-start(s32[2,80,5]{1,0,2:T(2,128)} %param.6) | copy-start | bytes 9604
  59.5 32.2 %all-to-all-start = ((f32[2,80,2,160]{3,2,0,1:T(2,128)}), f32[2,80,2,160]{3,2,0,1:T(2,128)S(1)}, u32[]{:S(2)}, u32[]{:S(2)}) async-start(f32[2,80,2,160]{3,2,0,1:T(2,128)} %copy.144), calls=%async_computation | async-start | bytes 655360 | tf_op jit(solution)/shard_map/all_to_all | solution.py:152
  113.4 11.2 %all-to-all-start.1 = ((f32[4,1,12800]{2,1,0:T(1,128)}), f32[4,1,12800]{2,1,0:T(1,128)S(1)}, u32[]{:S(2)}, u32[]{:S(2)}) async-start(f32[4,1,12800]{2,1,0:T(1,128)} %reshape.494), calls=%async_computation.1 | async-start | bytes 409600 | tf_op jit(solution)/shard_map/all_to_all | solution.py:43
  129.4 10.8 %all-to-all-start.2 = ((f32[4,1,12800]{2,1,0:T(1,128)}), f32[4,1,12800]{2,1,0:T(1,128)S(1)}, u32[]{:S(2)}, u32[]{:S(2)}) async-start(f32[4,1,12800]{2,1,0:T(1,128)} %reshape.496), calls=%async_computation.2 | async-start | bytes 409600 | tf_op jit(solution)/shard_map/all_to_all | solution.py:43
  156.1 7.6 %copy-start.1 = (f32[2]{0:T(128)S(1)}, f32[2]{0:T(128)}, u32[]{:S(2)}) copy-start(f32[2]{0:T(128)} %param.9) | copy-start | bytes 28
  158.3 19.7 %all-to-all-start.3 = ((f32[8,2,2,5,1281]{4,2,1,3,0:T(2,128)}), f32[8,2,2,5,1281]{4,2,1,3,0:T(2,128)S(1)}, u32[]{:S(2)}, u32[]{:S(2)}) async-start(f32[8,2,2,5,1281]{4,2,1,3,0:T(2,128)} %bitcast.24), calls=%async_computation.3 | async-start | bytes 1802240 | tf_op jit(solution)/shard_map/all_to_all | solution.py:54
  179.6 32.0 %all-to-all-start.4 = ((f32[8,2,2,5,1281]{4,2,1,3,0:T(2,128)}), f32[8,2,2,5,1281]{4,2,1,3,0:T(2,128)S(1)}, u32[]{:S(2)}, u32[]{:S(2)}) async-start(f32[8,2,2,5,1281]{4,2,1,3,0:T(2,128)} %broadcast_in_dim.102), calls=%async_computation.4 | async-start | bytes 1802240 | tf_op jit(solution)/shard_map/all_to_all | solution.py:60
  237.4 33.5 %all-to-all-start.5 = ((f32[16,1,3200]{2,1,0:T(1,128)}), f32[16,1,3200]{2,1,0:T(1,128)S(1)}, u32[]{:S(2)}, u32[]{:S(2)}) async-start(f32[16,1,3200]{2,1,0:T(1,128)} %reshape.498), calls=%async_computation.5 | async-start | bytes 409600 | tf_op jit(solution)/shard_map/all_to_all | solution.py:173
where the time goes:
time: 345 us; the launch traced here: 338 us
  other arithmetic  125 us (36%)
  matrix products  82.5 us (24%)
  local copies, waits for them, and re-layouts  55.1 us (16%)
  starting transfers between devices  31.8 us (9%)
  waiting for transfers between devices  26.6 us (8%)
  blocking collectives  15.7 us (5%)
    unnamed x14, local copies, waits for them, and re-layouts  34.9 us
    mul x1, other arithmetic, inverse_table(): 2.0 * jnp.cos(upper_angle)  29.7 us
    cos x1, other arithmetic, forward_table(): jnp.cos(upper_angle)  28.3 us
    mul x1, other arithmetic, inverse_table(): -lower_scale * jnp.sin(lower_angle)  28.3 us
    neg x1, other arithmetic, forward_table(): -jnp.sin(lower_angle)  27.9 us
    dot_general x1, matrix products, synthesise(): return jnp.einsum('hvcpk,plk->hvcpl', stacked, legendre, precision=HIGHEST)  20.8 us
    dot_general x1, matrix products, local(): jnp.einsum('hlvn,ncp->hvcpl', columns, forward_table(lon_count, m_count,...  19 us
    dot_general x1, matrix products, local(): jnp.einsum('hvcpl,cpn->hlvn', returned, inverse_table(lon_count, m_count,...  17.7 us
  transfers between devices with their start and end apart: 8, of which 3 were waited for; matrix products, arithmetic and copies ran while one was open for 37% of the time, Pallas kernels for 0%

commit v1 on v0

v1 whole, which is shorter than its diff:
```python
import math

import jax
import jax.numpy as jnp
import ml_dtypes
import numpy as np
from jax import lax
from jax.experimental import pallas as pl
from jax.experimental.pallas import tpu as pltpu
from jax.sharding import PartitionSpec as P

F32 = jnp.float32
BF16 = jnp.bfloat16
LON = 2560
WAVES = 1280
ROWS = WAVES + 1
TILE = 32
LANES = 128
LAT = 80
BLOCK = 40
SHARE = 5
TILES = 5


def halves(table):
    high = table.astype(ml_dtypes.bfloat16)
    low = (table - high.astype(np.float64)).astype(ml_dtypes.bfloat16)
    return high, low


def tables():
    cls = np.arange(4)[:, None, None]
    d = np.arange(16)[None, :, None]
    j = np.arange(10)[None, None, :]
    lower = BLOCK * d + 4 * j + cls
    upper = WAVES - 4 - BLOCK * d - 4 * j + cls
    m = np.stack([lower, upper], axis=2)
    xi = np.arange(640)
    angle = 2.0 * math.pi / LON * ((m[..., None] * xi) % LON)
    cos, sin = np.cos(angle), np.sin(angle)
    sign = np.where(np.arange(4) == 3, -1.0, 1.0)[:, None, None, None, None]
    real = np.concatenate([cos, sin * sign], axis=-1)
    imag = np.concatenate([-sin, cos * sign], axis=-1)
    forward = np.stack([real, imag], axis=4).reshape(4, 640, 1280) / LON
    scale = np.where(m == 0, 1.0, 2.0)[..., None]
    cos, sin = cos * scale, sin * scale
    real = np.stack([cos, -sin], axis=4).reshape(4, 640, 640)
    imag = np.stack([sin, cos], axis=4).reshape(4, 640, 640)
    both = np.stack([real, imag], axis=1)
    both = both.reshape(4, 2, 640, 4, 160).transpose(0, 3, 1, 4, 2)
    inverse = both.reshape(4, 1280, 640)
    return forward, inverse


def split(value):
    high = value.astype(BF16)
    low = (value - high.astype(F32)).astype(BF16)
    return high, low


def dot(a, b):
    return jnp.dot(a, b, preferred_element_type=F32)


def dot_t(a, b):
    return lax.dot_general(a, b, (((1,), (1,)), ((), ())), preferred_element_type=F32)


def remote(src, dst, send, recv, device):
    return pltpu.make_async_remote_copy(
        src_ref=src,
        dst_ref=dst,
        send_sem=send,
        recv_sem=recv,
        device_id=device,
        device_id_type=pl.DeviceIdType.MESH,
    )


def kernel(
    field,
    depart,
    weight,
    legendre,
    damping,
    fwd_high,
    fwd_low,
    inv_high,
    inv_low,
    out,
    ext,
    wbuf,
    win,
    adv,
    r1,
    s2,
    r2,
    zc,
    fh,
    fl,
    ih,
    il,
    s3,
    r3,
    eo,
    lf,
    lb,
    legf,
    legh,
    legl,
    pbuf,
    cbuf,
    sbuf,
    tbuf,
    gbuf,
    syn,
    s4,
    r4,
    yc,
    s5,
    r5,
    o6,
    local_sem,
    w_sem,
    leg_sem,
    tab_sem,
    halo_s,
    halo_r,
    e1_s,
    e1_r,
    e2_s,
    e2_r,
    e3_s,
    e3_r,
    c1_s,
    c1_r,
    c2_s,
    c2_r,
    gz_s,
    gz_r,
    gp_s,
    gp_r,
    e4_s,
    e4_r,
    e5_s,
    e5_r,
    e6_s,
    e6_r,
):
    band = lax.axis_index("band")
    sec = lax.axis_index("sector")
    y, x = sec // 4, sec % 4
    z, core = band // 2, band % 2
    odd = x % 2 == 1

    own = pltpu.make_async_copy(field, ext.at[:, :, pl.ds(64, 160), :], local_sem)
    own.start()

    def w_copy(h, t):
        return pltpu.make_async_copy(weight.at[h, t], wbuf.at[h, t], w_sem.at[h, t])

    @pl.loop(0, TILES)
    def _(t):
        for h in range(2):
            w_copy(h, t).start()

    loads = [
        pltpu.make_async_copy(src.at[x], dst, tab_sem.at[i])
        for i, (src, dst) in enumerate(
            [(fwd_high, fh), (fwd_low, fl), (inv_high, ih), (inv_low, il)]
        )
    ]
    loads[0].start()
    loads[1].start()

    def leg_copy(q):
        rows = pl.ds(q * SHARE, SHARE)
        return pltpu.make_async_copy(legendre.at[rows], legf.at[rows], leg_sem.at[q])

    @pl.loop(0, 8)
    def _(q):
        leg_copy(q).start()

    loads[2].start()
    loads[3].start()

    barrier = pltpu.get_barrier_semaphore()

    def greet(device):
        pl.semaphore_signal(barrier, inc=1, device_id=device, device_id_type=pl.DeviceIdType.MESH)

    for k in range(1, 16):
        greet((band, (sec + k) % 16))
    for k in range(1, 4):
        greet((((z + k) % 4) * 2 + core, sec))
    greet((z * 2 + 1 - core, sec))
    pl.semaphore_wait(barrier, 19)

    right, left = (sec + 1) % 16, (sec + 15) % 16
    to_right = remote(
        field.at[:, :, pl.ds(96, 64), :],
        ext.at[:, :, pl.ds(0, 64), :],
        halo_s.at[0],
        halo_r.at[0],
        (band, right),
    )
    to_left = remote(
        field.at[:, :, pl.ds(0, 96), :],
        ext.at[:, :, pl.ds(224, 96), :],
        halo_s.at[1],
        halo_r.at[1],
        (band, left),
    )
    to_right.start()
    to_left.start()
    adv[...] = jnp.zeros_like(adv)

    @pl.when(jnp.logical_not(odd))
    def _():
        r2[1] = jnp.zeros_like(r2[1])

    own.wait()
    to_right.wait_recv()
    to_left.wait_recv()

    def e1(t, k):
        to = (y + k) % 4
        return remote(
            adv.at[to, t], r1.at[y, t], e1_s.at[t, k], e1_r.at[t, y], (band, to * 4 + x)
        )

    def e1_arrives(t, k):
        source = (y + k) % 4
        remote(
            adv.at[source, t],
            r1.at[source, t],
            e1_s.at[t, k],
            e1_r.at[t, source],
            (band, source * 4 + x),
        ).wait_recv()

    def e2(t, k, part):
        to = (x + k) % 4
        src = s2.at[3, t] if part else s2.at[to - 2 * (to // 3), t]
        return remote(
            src,
            r2.at[part, x, t],
            e2_s.at[part, t, k],
            e2_r.at[part, t, x],
            (band, y * 4 + to),
        )

    def e2_arrives(t, k, part):
        source = (x + k) % 4
        remote(
            s2.at[0, t],
            r2.at[part, source, t],
            e2_s.at[part, t, k],
            e2_r.at[part, t, source],
            (band, y * 4 + source),
        ).wait_recv()

    def advect(t):
        for h in range(2):
            w_copy(h, t).wait()
            dep = depart[t, h : h + 1, :]
            for v in range(2):
                window = ext[h, v, pl.ds(pl.multiple_of(t * TILE, TILE), 64), 0:LAT]
                for offset in range(-1, 3):
                    start = pl.multiple_of((t + offset + 2) * TILE, TILE)
                    candidate = ext[h, v, pl.ds(start, 64), 0:LAT]
                    window = jnp.where(dep == offset, candidate, window)
                win[v] = window
            total = [jnp.zeros((TILE, LAT), F32) for _ in range(2)]
            for j in range(64):
                w = wbuf[h, t, j].astype(F32)
                for v in range(2):
                    total[v] = total[v] + win[v, j : j + 1, :] * w
            for v in range(2):
                adv[h * 2 + v, t, :, 0:LAT] = total[v]
        for k in range(1, 4):
            e1(t, k).start()
        r1[y, t] = adv[y, t]

    def radix(t):
        for k in range(1, 4):
            e1_arrives(t, k)
        a, b, c, d = r1[0, t], r1[1, t], r1[2, t], r1[3, t]
        s2[0, t] = (a + c) + (b + d)
        s2[1, t] = a - c
        s2[2, t] = (a + c) - (b + d)
        s2[3, t] = d - b
        for k in range(1, 4):
            e2(t, k, 0).start()

            @pl.when((x + k) % 2 == 1)
            def _():
                e2(t, k, 1).start()

        r2[0, x, t] = s2[x - 2 * (x // 3), t]

        @pl.when(odd)
        def _():
            r2[1, x, t] = s2[3, t]

    @pl.loop(0, TILES + 1)
    def _(t):
        @pl.when(t < TILES)
        def _():
            advect(t)

        @pl.when(t > 0)
        def _():
            radix(t - 1)

    @pl.loop(0, TILES)
    def _(t):
        for k in range(1, 4):
            e2_arrives(t, k, 0)

            @pl.when(odd)
            def _():
                e2_arrives(t, k, 1)

    @pl.loop(0, 8)
    def _(i):
        part, source = i // 4, i % 4
        for t in range(TILES):
            high, low = split(r2[part, source, t])
            start = pl.multiple_of(i * 160 + t * TILE, TILE)
            zc[pl.ds(start, TILE), 0:LANES] = high
            zc[pl.ds(start, TILE), LANES : 2 * LANES] = low

    loads[0].wait()
    loads[1].wait()

    def e3(d):
        return remote(s3.at[d], r3.at[sec], e3_s.at[d], e3_r.at[sec], (band, d))

    @pl.loop(0, 4)
    def _(g):
        group = (g + sec // 4) % 4
        rows = pl.ds(pl.multiple_of(group * 160, 160), 160)
        both = dot(fh[rows, :], zc[...])
        value = both[:, 0:LANES] + both[:, LANES:] + dot(fl[rows, :], zc[:, 0:LANES])
        for q in range(4):
            d = group * 4 + q
            s3[d] = value[q * BLOCK : (q + 1) * BLOCK]

            @pl.when(d != sec)
            def _():
                e3(d).start()

            @pl.when(d == sec)
            def _():
                r3[d] = value[q * BLOCK : (q + 1) * BLOCK]

    @pl.loop(0, 8)
    def _(q):
        leg_copy(q).wait()

        @pl.loop(0, SHARE * TILES)
        def _(i):
            p = q * SHARE + i // 5
            rows = pl.ds(pl.multiple_of((i % 5) * 16, 16), 16)
            high, low = split(legf[p, rows, :])
            legh[p, rows, :] = high
            legl[p, rows, :] = low

    @pl.loop(1, 16)
    def _(k):
        source = (sec + k) % 16
        remote(
            s3.at[source], r3.at[source], e3_s.at[source], e3_r.at[source], (band, source)
        ).wait_recv()

    for v in range(2):
        for c in range(4):
            north, south = r3[v * 4 + c], r3[8 + v * 4 + c]
            eo[0, v, c] = north + south
            eo[1, v, c] = north - south
    for p in range(BLOCK):
        j, c = p // 4, p % 4
        for s in range(2):
            for v in range(2):
                row = s * 8 + v * 2
                lf[p, row : row + 2, :] = eo[s, v, c, 2 * j : 2 * j + 2, :]
                lf[p, row + 4 : row + 6, :] = eo[s, v, 3 - c, 20 + 2 * j : 22 + 2 * j, :]

    @pl.loop(0, BLOCK)
    def _(p):
        high, low = split(lf[p])
        lb[p, 0:16, :] = high
        lb[p, 16:32, :] = low

    column = lax.broadcasted_iota(jnp.int32, (8, ROWS), 1)

    def masks(p):
        limit = WAVES - (sec * BLOCK + p)
        leading = column < limit
        lag = jnp.where(leading, column, column - limit)
        return leading, (lag & 1) == 1

    def analyse(share, i):
        p = share * SHARE + i
        lhs = lb[p, :, 0:LAT]
        both = dot(lhs, legh[p])
        total = both[0:16] + both[16:32] + dot(lhs[0:16], legl[p])
        leading, odd_rows = masks(p)
        chosen = jnp.where(odd_rows, total[8:16], total[0:8])
        return jnp.where(leading[0:4], chosen[0:4], chosen[4:8])

    partner = (z * 2 + 1 - core, sec)

    def c1(to):
        return remote(pbuf.at[to], cbuf.at[to], c1_s.at[to], c1_r.at[to], partner)

    @pl.loop(0, 4)
    def _(k):
        to = (z + 1 + k) % 4

        @pl.loop(0, SHARE)
        def _(i):
            pbuf[to, i] = analyse(to * 2 + 1 - core, i)

        c1(to).start()

    def c2(to):
        return remote(sbuf.at[to], tbuf.at[z], c2_s.at[to], c2_r.at[z], (to * 2 + core, sec))

    @pl.loop(0, 4)
    def _(k):
        to = (z + 1 + k) % 4

        @pl.loop(0, SHARE)
        def _(i):
            sbuf[to, i] = analyse(to * 2 + core, i)

        c1(to).wait_recv()

        @pl.loop(0, SHARE)
        def _(i):
            sbuf[to, i] = sbuf[to, i] + cbuf[to, i]

        @pl.when(to != z)
        def _():
            c2(to).start()

    for k in range(1, 4):
        source = (z + k) % 4
        remote(
            sbuf.at[source],
            tbuf.at[source],
            c2_s.at[source],
            c2_r.at[source],
            (source * 2 + core, sec),
        ).wait_recv()

    tbuf[z] = sbuf[z]
    first_level = lax.broadcasted_iota(jnp.int32, (4, ROWS), 0) < 2
    level = jnp.where(first_level, damping[0], damping[1])

    @pl.loop(0, SHARE)
    def _(i):
        p = sec * BLOCK + band * SHARE + i
        column4 = column[0:4]
        degree = jnp.where(column4 < WAVES - p, p + column4, column4 - 1)
        ratio = (degree * (degree + 1)).astype(F32) / float(WAVES * WAVES)
        total = (tbuf[0, i] + tbuf[1, i]) + (tbuf[2, i] + tbuf[3, i])
        gbuf[band, i] = total / (1.0 + level * ratio)

    def gz(k):
        to = (z + k) % 4
        return remote(
            gbuf.at[band], gbuf.at[band], gz_s.at[k], gz_r.at[z], (to * 2 + core, sec)
        )

    def gz_arrives(source):
        share = source * 2 + core
        remote(
            gbuf.at[share], gbuf.at[share], gz_s.at[0], gz_r.at[source], (share, sec)
        ).wait_recv()

    def gp(source):
        share = source * 2 + core
        return remote(gbuf.at[share], gbuf.at[share], gp_s.at[source], gp_r.at[source], partner)

    def gp_arrives(source):
        share = source * 2 + 1 - core
        remote(
            gbuf.at[share], gbuf.at[share], gp_s.at[source], gp_r.at[source], partner
        ).wait_recv()

    for k in range(1, 4):
        gz(k).start()
    gp(z).start()

    def synthesise(share):
        @pl.loop(0, SHARE)
        def _(i):
            p = share * SHARE + i
            spec = gbuf[share, i]
            leading, odd_rows = masks(p)
            north = jnp.concatenate([spec, spec], axis=0)
            upper = lax.broadcasted_iota(jnp.int32, (8, ROWS), 0) >= 4
            north = jnp.where(leading != upper, north, 0.0)
            south = jnp.where(odd_rows, -north, north)
            high, low = split(jnp.concatenate([north, south], axis=0))
            both = dot_t(jnp.concatenate([high, low], axis=0), legh[p])
            syn[p, :, 0:LAT] = both[0:16] + both[16:32] + dot_t(high, legl[p])

    synthesise(band)
    gp_arrives(z)
    synthesise(z * 2 + 1 - core)

    @pl.loop(1, 4)
    def _(k):
        source = (z + k) % 4
        gz_arrives(source)
        gp(source).start()
        synthesise(source * 2 + core)

    @pl.loop(1, 4)
    def _(k):
        source = (z + k) % 4
        gp_arrives(source)
        synthesise(source * 2 + 1 - core)

    for p in range(BLOCK):
        j, c = p // 4, p % 4
        for h in range(2):
            for v in range(2):
                row = h * 8 + v * 2
                block = (h * 2 + v) * 4
                s4[block + c, 2 * j : 2 * j + 2, :] = syn[p, row : row + 2, :]
                s4[block + 3 - c, 20 + 2 * j : 22 + 2 * j, :] = syn[p, row + 4 : row + 6, :]

    def e4(k):
        to = (sec + k) % 16
        return remote(s4.at[to], r4.at[sec], e4_s.at[k], e4_r.at[sec], (band, to))

    @pl.loop(1, 16)
    def _(k):
        e4(k).start()

    r4[sec] = s4[sec]
    loads[2].wait()
    loads[3].wait()

    @pl.loop(1, 16)
    def _(k):
        source = (sec + k) % 16
        remote(
            s4.at[source], r4.at[source], e4_s.at[k], e4_r.at[source], (band, source)
        ).wait_recv()

    @pl.loop(0, 8)
    def _(i):
        pair = jnp.concatenate([r4[2 * i], r4[2 * i + 1]], axis=0)
        high, low = split(pair)
        start = pl.multiple_of(i * 80, 80)
        yc[pl.ds(start, 80), 0:LANES] = high
        yc[pl.ds(start, 80), LANES : 2 * LANES] = low

    def e5(k, part):
        to = (x + k) % 4
        return remote(
            s5.at[part, to],
            r5.at[part, x],
            e5_s.at[part, k],
            e5_r.at[part, x],
            (band, y * 4 + to),
        )

    def e5_arrives(k, part):
        source = (x + k) % 4
        remote(
            s5.at[part, source],
            r5.at[part, source],
            e5_s.at[part, k],
            e5_r.at[part, source],
            (band, y * 4 + source),
        ).wait_recv()

    @pl.loop(0, 4)
    def _(g):
        k = (g + 1) % 4
        to = (x + k) % 4

        def part_of(part):
            rows = pl.ds(pl.multiple_of((to * 2 + part) * 160, 160), 160)
            both = dot(ih[rows, :], yc[...])
            value = both[:, 0:LANES] + both[:, LANES:] + dot(il[rows, :], yc[:, 0:LANES])
            s5[part, to] = value

            @pl.when(k != 0)
            def _():
                e5(k, part).start()

            @pl.when(k == 0)
            def _():
                r5[part, to] = value

        part_of(0)

        @pl.when(odd)
        def _():
            part_of(1)

    for k in range(1, 4):
        e5_arrives(k, 0)

        @pl.when((x + k) % 2 == 1)
        def _():
            e5_arrives(k, 1)

    def e6(t, k):
        to = (y + k) % 4
        return remote(
            o6.at[to, t], out.at[y, t], e6_s.at[t, k], e6_r.at[t, y], (band, to * 4 + x)
        )

    @pl.loop(0, TILES)
    def _(t):
        rows = pl.ds(pl.multiple_of(t * TILE, TILE), TILE)
        a, c = r5[0, 0, rows, :], r5[0, 2, rows, :]
        b = r5[0, 1, rows, :] + r5[0, 3, rows, :]
        d = r5[1, 3, rows, :] - r5[1, 1, rows, :]
        o6[0, t] = (a + c) + b
        o6[1, t] = (a - c) + d
        o6[2, t] = (a + c) - b
        o6[3, t] = (a - c) - d
        for k in range(1, 4):
            e6(t, k).start()
        out[y, t] = o6[y, t]

    @pl.loop(0, TILES)
    def _(t):
        for k in range(1, 4):
            source = (y + k) % 4
            remote(
                o6.at[source, t],
                out.at[source, t],
                e6_s.at[t, k],
                e6_r.at[t, source],
                (band, source * 4 + x),
            ).wait_recv()

    to_right.wait_send()
    to_left.wait_send()

    @pl.loop(0, TILES)
    def _(t):
        for k in range(1, 4):
            e1(t, k).wait_send()
            e2(t, k, 0).wait_send()

            @pl.when((x + k) % 2 == 1)
            def _():
                e2(t, k, 1).wait_send()

            e6(t, k).wait_send()

    @pl.loop(1, 16)
    def _(k):
        e3((sec + k) % 16).wait_send()
        e4(k).wait_send()

    for k in range(4):
        c1((z + k) % 4).wait_send()
        gp(k).wait_send()
    for k in range(1, 4):
        c2((z + k) % 4).wait_send()
        gz(k).wait_send()
        e5(k, 0).wait_send()

        @pl.when(odd)
        def _():
            e5(k, 1).wait_send()


def local(field, depart, interp_weight, legendre, damping):
    moved = jnp.pad(jnp.transpose(field, (0, 2, 3, 1)), ((0, 0),) * 3 + ((0, LANES - LAT),))
    forward, inverse = tables()
    constants = [jnp.asarray(t) for t in (*halves(forward), *halves(inverse))]
    vmem = pl.BlockSpec(memory_space=pltpu.VMEM)
    hbm = pl.BlockSpec(memory_space=pl.ANY)
    scratch = [
        pltpu.VMEM((2, 2, 320, LANES), F32),
        pltpu.VMEM((2, 5, 64, TILE, LAT), BF16),
        pltpu.VMEM((2, 64, LAT), F32),
        pltpu.VMEM((4, 5, TILE, LANES), F32),
        pltpu.VMEM((4, 5, TILE, LANES), F32),
        pltpu.VMEM((4, 5, TILE, LANES), F32),
        pltpu.VMEM((2, 4, 5, TILE, LANES), F32),
        pltpu.VMEM((1280, 2 * LANES), BF16),
        pltpu.VMEM((640, 1280), BF16),
        pltpu.VMEM((640, 1280), BF16),
        pltpu.VMEM((1280, 640), BF16),
        pltpu.VMEM((1280, 640), BF16),
        pltpu.VMEM((16, BLOCK, LANES), F32),
        pltpu.VMEM((16, BLOCK, LANES), F32),
        pltpu.VMEM((2, 2, 4, BLOCK, LANES), F32),
        pltpu.VMEM((BLOCK, 16, LANES), F32),
        pltpu.VMEM((BLOCK, 32, LANES), BF16),
        pltpu.VMEM((BLOCK, LAT, ROWS), F32),
        pltpu.VMEM((BLOCK, LAT, ROWS), BF16),
        pltpu.VMEM((BLOCK, LAT, ROWS), BF16),
        pltpu.VMEM((4, SHARE, 4, ROWS), F32),
        pltpu.VMEM((4, SHARE, 4, ROWS), F32),
        pltpu.VMEM((4, SHARE, 4, ROWS), F32),
        pltpu.VMEM((4, SHARE, 4, ROWS), F32),
        pltpu.VMEM((8, SHARE, 4, ROWS), F32),
        pltpu.VMEM((BLOCK, 16, LANES), F32),
        pltpu.VMEM((16, BLOCK, LANES), F32),
        pltpu.VMEM((16, BLOCK, LANES), F32),
        pltpu.VMEM((640, 2 * LANES), BF16),
        pltpu.VMEM((2, 4, 160, LANES), F32),
        pltpu.VMEM((2, 4, 160, LANES), F32),
        pltpu.VMEM((4, 5, TILE, LANES), F32),
    ]
    dma = pltpu.SemaphoreType.DMA
    scratch += [
        dma,
        dma((2, 5)),
        dma((8,)),
        dma((4,)),
        dma((2,)),
        dma((2,)),
        dma((5, 4)),
        dma((5, 4)),
        dma((2, 5, 4)),
        dma((2, 5, 4)),
        dma((16,)),
        dma((16,)),
        dma((4,)),
        dma((4,)),
        dma((4,)),
        dma((4,)),
        dma((4,)),
        dma((4,)),
        dma((4,)),
        dma((4,)),
        dma((16,)),
        dma((16,)),
        dma((2, 4)),
        dma((2, 4)),
        dma((5, 4)),
        dma((5, 4)),
    ]
    grid = pl.pallas_call(
        kernel,
        out_shape=jax.ShapeDtypeStruct((4, 5, TILE, LANES), F32),
        in_specs=[vmem, vmem, hbm, hbm, pl.BlockSpec(memory_space=pltpu.SMEM)] + [hbm] * 4,
        out_specs=vmem,
        scratch_shapes=scratch,
        compiler_params=pltpu.CompilerParams(
            collective_id=0, has_side_effects=True, vmem_limit_bytes=62 * 1024 * 1024
        ),
    )(
        moved,
        jnp.transpose(depart, (2, 0, 1)),
        jnp.transpose(interp_weight, (0, 2, 3, 4, 1)),
        legendre,
        damping,
        *constants,
    )
    grid = grid.reshape(2, 2, 160, LANES)[..., 0:LAT]
    return jnp.transpose(grid, (0, 3, 1, 2))


def solution(mesh):
    placed = (
        P(None, "band", None, "sector"),
        P(None, "band", "sector"),
        P(None, "band", "sector", None, None),
        P("sector", "band", None),
        P(),
    )
    return jax.shard_map(
        local, mesh=mesh, in_specs=placed, out_specs=P(None, "band", None, "sector"), check_vma=False
    )
```

time: 345 us -> 92 us (0.27); the launches traced: 338 us -> 91.9 us
  other arithmetic: 125 us -> 0 us
  Pallas kernels: 0 us -> 88.1 us
  matrix products: 82.5 us -> 0 us
  local copies, waits for them, and re-layouts: 55.1 us -> 3.78 us
  starting transfers between devices: 31.8 us -> 0 us
  waiting for transfers between devices: 26.6 us -> 0 us
  blocking collectives: 15.7 us -> 0 us
    pallas_call x0 -> x1, Pallas kernels: none -> 88.1 us  [local(): pl.pallas_call(kernel, out_shape=jax.ShapeDtypeStruct((4, 5, TILE, LANES)...]
    dot_general x5 -> x0, matrix products: 82.5 us -> none  [the longest x1 20.8 us: synthesise(): return jnp.einsum('hvcpk,plk->hvcpl', stacked, legendre, precision=HIGHEST)]
    mul x2 -> x0, other arithmetic: 58 us -> none  [the longest x1 29.7 us: inverse_table(): 2.0 * jnp.cos(upper_angle)]
    unnamed x14 -> x2, local copies, waits for them, and re-layouts: 34.9 us -> 3.03 us
    cos x1 -> x0, other arithmetic: 28.3 us -> none  [forward_table(): jnp.cos(upper_angle)]
    neg x2 -> x0, other arithmetic: 27.9 us -> none  [the longest x1 27.9 us: forward_table(): -jnp.sin(lower_angle)]
    all_to_all x6 -> x0, waiting for transfers between devices: 26.6 us -> none  [the longest x1 14.2 us: summed_on_arrival(): pieces = lax.all_to_all(split_up(x, dim, peers), axis, 0, 0, tiled=True)]
    all_to_all x6 -> x0, starting transfers between devices: 26.3 us -> none  [the longest x2 9.2 us: moved_by_axis(): lax.all_to_all(pieces, axes[k], split_axis=k, concat_axis=k, tiled=True)]
  transfers between devices with their start and end apart: 8 -> 0, of which waited for: 3 -> 0; matrix products, arithmetic and copies ran while one was open for 37% -> 0% of each run, Pallas kernels for 0% -> 0%
where the time goes in v1:
time: 92 us; the launch traced here: 91.9 us
  Pallas kernels  88.1 us (96%)
  local copies, waits for them, and re-layouts  3.78 us (4%)
    pallas_call x1, Pallas kernels, local(): pl.pallas_call(kernel, out_shape=jax.ShapeDtypeStruct((4, 5, TILE, LANES)...  88.1 us
    unnamed x2, local copies, waits for them, and re-layouts  3.03 us

profile of v1, /device:TPU:0, one launch (start us, length us, event | category | flops | bytes accessed | tf_op | source)
XLA Modules:
  0.0 91.9 jit_solution(509219900855126266)
XLA Ops:
  0.0 1.1 %copy.10 = f32[2,80,2,160]{1,3,2,0:T(8,128)S(1)} copy(f32[2,80,2,160]{3,2,1,0:T(2,128)} %param.9) | data formatting | bytes 409600 | tf_op args[0]
  1.1 0.8 pad.4.field
  1.9 88.1 %shard_map.91 = f32[4,5,32,128]{3,2,1,0:T(8,128)} custom-call(f32[2,2,160,128]{3,2,1,0:T(8,128)} %pad.4.field, s32[5,2,80]{2,1,0:T(2,128)} %bitcast.9, bf16[2,5,64,32,80]{4,3,2,1,0:T(8,128)(2,1)} %bitcast.6, f32[40,80,1281]{2,1,0:T(8,128)} %legendre.1, f32[2]{0:T(128)} %damping.1, bf16[4,640,1280]{2,1,0:T(8,128)(2,1)} %constant.11.clone.fwd_high, ...), custom_call_target="tpu_custom_call" | custom-call | tf_op jit(solution)/shard_map/pallas_call | solution.py:751
  90.0 1.9 %copy.12 = f32[2,2,160,80]{2,1,3,0:T(2,128)} copy(f32[2,2,160,80]{3,2,1,0:T(8,128)} %bitcast.7) | data formatting | bytes 409600

commit v2 on v1

--- a/solution.py
+++ b/solution.py
@@ -14,6 +14,7 @@
 LON = 2560
 WAVES = 1280
 ROWS = WAVES + 1
+WIDE = WAVES + 128
 TILE = 32
 LANES = 128
 LAT = 80
@@ -111,6 +112,7 @@
     pbuf,
     cbuf,
     sbuf,
+    rbuf,
     tbuf,
     gbuf,
     syn,
@@ -177,13 +179,6 @@
         rows = pl.ds(q * SHARE, SHARE)
         return pltpu.make_async_copy(legendre.at[rows], legf.at[rows], leg_sem.at[q])
 
-    @pl.loop(0, 8)
-    def _(q):
-        leg_copy(q).start()
-
-    loads[2].start()
-    loads[3].start()
-
     barrier = pltpu.get_barrier_semaphore()
 
     def greet(device):
@@ -222,6 +217,11 @@
     own.wait()
     to_right.wait_recv()
     to_left.wait_recv()
+
+    @pl.loop(0, 8)
+    def _(q):
+        leg_copy(q).start(priority=1)
+
 
     def e1(t, k):
         to = (y + k) % 4
@@ -303,15 +303,8 @@
         def _():
             r2[1, x, t] = s2[3, t]
 
-    @pl.loop(0, TILES + 1)
-    def _(t):
-        @pl.when(t < TILES)
-        def _():
-            advect(t)
-
-        @pl.when(t > 0)
-        def _():
-            radix(t - 1)
+    pl.loop(0, TILES)(advect)
+    pl.loop(0, TILES)(radix)
 
     @pl.loop(0, TILES)
     def _(t):
@@ -354,6 +347,9 @@
             @pl.when(d == sec)
             def _():
                 r3[d] = value[q * BLOCK : (q + 1) * BLOCK]
+
+    loads[2].start()
+    loads[3].start()
 
     @pl.loop(0, 8)
     def _(q):
@@ -401,62 +397,74 @@
         lag = jnp.where(leading, column, column - limit)
         return leading, (lag & 1) == 1
 
-    def analyse(share, i):
-        p = share * SHARE + i
-        lhs = lb[p, :, 0:LAT]
-        both = dot(lhs, legh[p])
-        total = both[0:16] + both[16:32] + dot(lhs[0:16], legl[p])
-        leading, odd_rows = masks(p)
-        chosen = jnp.where(odd_rows, total[8:16], total[0:8])
-        return jnp.where(leading[0:4], chosen[0:4], chosen[4:8])
+    def analyse(share):
+        results = []
+        for i in range(SHARE):
+            p = share * SHARE + i
+            lhs = lb[p, :, 0:LAT]
+            both = dot(lhs, legh[p])
+            total = both[0:16] + both[16:32] + dot(lhs[0:16], legl[p])
+            leading, odd_rows = masks(p)
+            chosen = jnp.where(odd_rows, total[8:16], total[0:8])
+            results.append(jnp.where(leading[0:4], chosen[0:4], chosen[4:8]))
+        return results
 
     partner = (z * 2 + 1 - core, sec)
-
-    def c1(to):
-        return remote(pbuf.at[to], cbuf.at[to], c1_s.at[to], c1_r.at[to], partner)
+    ahead, behind, across = (z + 1) % 4, (z + 3) % 4, (z + 2) % 4
+    up, down = (ahead * 2 + core, sec), (behind * 2 + core, sec)
+
+    def c1(k):
+        return remote(pbuf.at[k], cbuf.at[k], c1_s.at[k], c1_r.at[k], partner)
+
+    def share_at(k, which):
+        return ((z + 2 + 3 * k + 3 * (k // 2) + 2 * (k // 3)) % 4) * 2 + which
 
     @pl.loop(0, 4)
     def _(k):
-        to = (z + 1 + k) % 4
-
-        @pl.loop(0, SHARE)
-        def _(i):
-            pbuf[to, i] = analyse(to * 2 + 1 - core, i)
-
-        c1(to).start()
-
-    def c2(to):
-        return remote(sbuf.at[to], tbuf.at[z], c2_s.at[to], c2_r.at[z], (to * 2 + core, sec))
+        for i, value in enumerate(analyse(share_at(k, 1 - core))):
+            pbuf[k, i, :, 0:ROWS] = value
+        c1(k).start()
+
+    first, last = pl.ds(0, 3), pl.ds(3, 2)
+    half_up = remote(sbuf.at[0, first], rbuf.at[first], c2_s.at[0], c2_r.at[0], up)
+    half_down = remote(sbuf.at[0, last], rbuf.at[last], c2_s.at[1], c2_r.at[1], down)
+    early_up = remote(sbuf.at[1, last], tbuf.at[0, last], c2_s.at[2], c2_r.at[2], up)
+    early_down = remote(sbuf.at[2, first], tbuf.at[1, first], c2_s.at[3], c2_r.at[3], down)
+    late_up = remote(sbuf.at[1, first], tbuf.at[0, first], c2_s.at[4], c2_r.at[4], up)
+    late_down = remote(sbuf.at[2, last], tbuf.at[1, last], c2_s.at[5], c2_r.at[5], down)
 
     @pl.loop(0, 4)
     def _(k):
-        to = (z + 1 + k) % 4
-
-        @pl.loop(0, SHARE)
-        def _(i):
-            sbuf[to, i] = analyse(to * 2 + core, i)
-
-        c1(to).wait_recv()
-
-        @pl.loop(0, SHARE)
-        def _(i):
-            sbuf[to, i] = sbuf[to, i] + cbuf[to, i]
-
-        @pl.when(to != z)
-        def _():
-            c2(to).start()
-
-    for k in range(1, 4):
-        source = (z + k) % 4
-        remote(
-            sbuf.at[source],
-            tbuf.at[source],
-            c2_s.at[source],
-            c2_r.at[source],
-            (source * 2 + core, sec),
-        ).wait_recv()
-
-    tbuf[z] = sbuf[z]
+        values = analyse(share_at(k, core))
+        for i, value in enumerate(values):
+            sbuf[k, i, :, 0:ROWS] = value
+        c1(k).wait_recv()
+        for i in range(SHARE):
+            sbuf[k, i] = sbuf[k, i] + cbuf[k, i]
+
+        @pl.when(k == 0)
+        def _():
+            half_up.start()
+            half_down.start()
+
+        @pl.when(k == 1)
+        def _():
+            early_up.start()
+
+        @pl.when(k == 2)
+        def _():
+            early_down.start()
+            half_up.wait_recv()
+            for i in range(3):
+                sbuf[1, i] = sbuf[1, i] + rbuf[i]
+            late_up.start()
+            half_down.wait_recv()
+            for i in range(3, SHARE):
+                sbuf[2, i] = sbuf[2, i] + rbuf[i]
+            late_down.start()
+
+    for copy in (early_up, early_down, late_up, late_down):
+        copy.wait_recv()
     first_level = lax.broadcasted_iota(jnp.int32, (4, ROWS), 0) < 2
     level = jnp.where(first_level, damping[0], damping[1])
 
@@ -466,65 +474,105 @@
         column4 = column[0:4]
         degree = jnp.where(column4 < WAVES - p, p + column4, column4 - 1)
         ratio = (degree * (degree + 1)).astype(F32) / float(WAVES * WAVES)
-        total = (tbuf[0, i] + tbuf[1, i]) + (tbuf[2, i] + tbuf[3, i])
-        gbuf[band, i] = total / (1.0 + level * ratio)
-
-    def gz(k):
-        to = (z + k) % 4
-        return remote(
-            gbuf.at[band], gbuf.at[band], gz_s.at[k], gz_r.at[z], (to * 2 + core, sec)
-        )
-
-    def gz_arrives(source):
-        share = source * 2 + core
-        remote(
-            gbuf.at[share], gbuf.at[share], gz_s.at[0], gz_r.at[source], (share, sec)
-        ).wait_recv()
-
-    def gp(source):
-        share = source * 2 + core
-        return remote(gbuf.at[share], gbuf.at[share], gp_s.at[source], gp_r.at[source], partner)
-
-    def gp_arrives(source):
-        share = source * 2 + 1 - core
-        remote(
-            gbuf.at[share], gbuf.at[share], gp_s.at[source], gp_r.at[source], partner
-        ).wait_recv()
-
-    for k in range(1, 4):
-        gz(k).start()
-    gp(z).start()
+        total = (tbuf[0, i] + tbuf[1, i]) + sbuf[3, i]
+        gbuf[band, i, :, 0:ROWS] = total[:, 0:ROWS] / (1.0 + level * ratio)
+
+    def gathered(share, rows, sem, to, send, recv):
+        ref = gbuf.at[share, rows]
+        return remote(ref, ref, send.at[sem], recv.at[sem], to)
+
+    every = pl.ds(0, SHARE)
+
+    def gz(sem, share, rows, to):
+        return gathered(share, rows, sem, to, gz_s, gz_r)
+
+    def gp(sem, share, rows):
+        return gathered(share, rows, sem, partner, gp_s, gp_r)
+
+    other = 1 - core
+    sends = [
+        gz(0, band, first, up),
+        gz(1, band, last, down),
+        gz(2, behind * 2 + core, first, up),
+        gz(3, ahead * 2 + core, last, down),
+        gz(4, band, last, up),
+        gz(5, band, first, down),
+        gp(0, band, every),
+        gp(1, behind * 2 + core, every),
+        gp(2, ahead * 2 + core, every),
+        gp(3, across * 2 + core, first),
+        gp(4, across * 2 + core, last),
+    ]
+    arrivals = [
+        gz(0, behind * 2 + core, first, up),
+        gz(1, ahead * 2 + core, last, down),
+        gz(2, across * 2 + core, first, up),
+        gz(3, across * 2 + core, last, down),
+        gz(4, behind * 2 + core, last, up),
+        gz(5, ahead * 2 + core, first, down),
+        gp(0, z * 2 + other, every),
+        gp(1, behind * 2 + other, every),
+        gp(2, ahead * 2 + other, every),
+        gp(3, across * 2 + other, first),
+        gp(4, across * 2 + other, last),
+    ]
+    for k in (0, 1, 4, 5, 6):
+        sends[k].start()
+    upper = lax.broadcasted_iota(jnp.int32, (8, ROWS), 0) >= 4
 
     def synthesise(share):
-        @pl.loop(0, SHARE)
-        def _(i):
+        for i in range(SHARE):
             p = share * SHARE + i
-            spec = gbuf[share, i]
+            spec = gbuf[share, i, :, 0:ROWS]
             leading, odd_rows = masks(p)
             north = jnp.concatenate([spec, spec], axis=0)
-            upper = lax.broadcasted_iota(jnp.int32, (8, ROWS), 0) >= 4
             north = jnp.where(leading != upper, north, 0.0)
             south = jnp.where(odd_rows, -north, north)
             high, low = split(jnp.concatenate([north, south], axis=0))
             both = dot_t(jnp.concatenate([high, low], axis=0), legh[p])
             syn[p, :, 0:LAT] = both[0:16] + both[16:32] + dot_t(high, legl[p])
 
-    synthesise(band)
-    gp_arrives(z)
-    synthesise(z * 2 + 1 - core)
-
-    @pl.loop(1, 4)
+    def step_share(k):
+        late, turn = (k + 6) // 8, (k + 1) % 3
+        chip = (z + late * (3 + 2 * turn + 3 * (turn // 2))) % 4
+        swap = (k + 3) // 8 + (1 - late) * k
+        return chip * 2 + core + swap * (1 - 2 * core)
+
+    @pl.loop(0, 8)
     def _(k):
-        source = (z + k) % 4
-        gz_arrives(source)
-        gp(source).start()
-        synthesise(source * 2 + core)
-
-    @pl.loop(1, 4)
-    def _(k):
-        source = (z + k) % 4
-        gp_arrives(source)
-        synthesise(source * 2 + 1 - core)
+        @pl.when(k == 1)
+        def _():
+            arrivals[6].wait_recv()
+
+        @pl.when(k == 2)
+        def _():
+            for n in (0, 1):
+                arrivals[n].wait_recv()
+                sends[n + 2].start()
+            for n in (4, 5):
+                arrivals[n].wait_recv()
+                sends[n + 3].start()
+
+        @pl.when(k == 4)
+        def _():
+            for n in (2, 3):
+                arrivals[n].wait_recv()
+                sends[n + 7].start()
+
+        @pl.when(k == 5)
+        def _():
+            arrivals[7].wait_recv()
+
+        @pl.when(k == 6)
+        def _():
+            arrivals[8].wait_recv()
+
+        @pl.when(k == 7)
+        def _():
+            arrivals[9].wait_recv()
+            arrivals[10].wait_recv()
+
+        synthesise(step_share(k))
 
     for p in range(BLOCK):
         j, c = p // 4, p % 4
@@ -667,11 +715,10 @@
         e4(k).wait_send()
 
     for k in range(4):
-        c1((z + k) % 4).wait_send()
-        gp(k).wait_send()
+        c1(k).wait_send()
+    for copy in (half_up, half_down, early_up, early_down, late_up, late_down, *sends):
+        copy.wait_send()
     for k in range(1, 4):
-        c2((z + k) % 4).wait_send()
-        gz(k).wait_send()
         e5(k, 0).wait_send()
 
         @pl.when(odd)
@@ -706,11 +753,12 @@
         pltpu.VMEM((BLOCK, LAT, ROWS), F32),
         pltpu.VMEM((BLOCK, LAT, ROWS), BF16),
         pltpu.VMEM((BLOCK, LAT, ROWS), BF16),
-        pltpu.VMEM((4, SHARE, 4, ROWS), F32),
-        pltpu.VMEM((4, SHARE, 4, ROWS), F32),
-        pltpu.VMEM((4, SHARE, 4, ROWS), F32),
-        pltpu.VMEM((4, SHARE, 4, ROWS), F32),
-        pltpu.VMEM((8, SHARE, 4, ROWS), F32),
+        pltpu.VMEM((4, SHARE, 4, WIDE), F32),
+        pltpu.VMEM((4, SHARE, 4, WIDE), F32),
+        pltpu.VMEM((4, SHARE, 4, WIDE), F32),
+        pltpu.VMEM((SHARE, 4, WIDE), F32),
+        pltpu.VMEM((2, SHARE, 4, WIDE), F32),
+        pltpu.VMEM((8, SHARE, 4, WIDE), F32),
         pltpu.VMEM((BLOCK, 16, LANES), F32),
         pltpu.VMEM((16, BLOCK, LANES), F32),
         pltpu.VMEM((16, BLOCK, LANES), F32),
@@ -735,12 +783,12 @@
         dma((16,)),
         dma((4,)),
         dma((4,)),
-        dma((4,)),
-        dma((4,)),
-        dma((4,)),
-        dma((4,)),
-        dma((4,)),
-        dma((4,)),
+        dma((6,)),
+        dma((6,)),
+        dma((6,)),
+        dma((6,)),
+        dma((5,)),
+        dma((5,)),
         dma((16,)),
         dma((16,)),
         dma((2, 4)),

time: 92 us -> 82.2 us (0.89)
  Pallas kernels: 88.1 us -> 77.9 us
    pallas_call x1, Pallas kernels: 88.1 us -> 77.9 us  [local(): pl.pallas_call(kernel, out_shape=jax.ShapeDtypeStruct((4, 5, TILE, LANES)...]
where the time goes in v2:
time: 82.2 us; the launch traced here: 81.7 us
  Pallas kernels  77.9 us (95%)
  local copies, waits for them, and re-layouts  3.78 us (5%)
    pallas_call x1, Pallas kernels, local(): pl.pallas_call(kernel, out_shape=jax.ShapeDtypeStruct((4, 5, TILE, LANES)...  77.9 us
    unnamed x2, local copies, waits for them, and re-layouts  3.03 us

profile of v2, /device:TPU:0, one launch (start us, length us, event | category | flops | bytes accessed | tf_op | source)
XLA Modules:
  0.0 81.7 jit_solution(9448239930478019466)
XLA Ops:
  0.0 1.1 %copy.10 = f32[2,80,2,160]{1,3,2,0:T(8,128)S(1)} copy(f32[2,80,2,160]{3,2,1,0:T(2,128)} %param.9) | data formatting | bytes 409600 | tf_op args[0]
  1.1 0.8 pad.4.field
  1.9 77.9 %shard_map.91 = f32[4,5,32,128]{3,2,1,0:T(8,128)} custom-call(f32[2,2,160,128]{3,2,1,0:T(8,128)} %pad.4.field, s32[5,2,80]{2,1,0:T(2,128)} %bitcast.9, bf16[2,5,64,32,80]{4,3,2,1,0:T(8,128)(2,1)} %bitcast.6, f32[40,80,1281]{2,1,0:T(8,128)} %legendre.1, f32[2]{0:T(128)} %damping.1, bf16[4,640,1280]{2,1,0:T(8,128)(2,1)} %constant.11.clone.fwd_high, ...), custom_call_target="tpu_custom_call" | custom-call | tf_op jit(solution)/shard_map/pallas_call | solution.py:799
  79.8 1.9 %copy.12 = f32[2,2,160,80]{2,1,3,0:T(2,128)} copy(f32[2,2,160,80]{3,2,1,0:T(8,128)} %bitcast.7) | data formatting | bytes 409600

commit v3 on v2

--- a/solution.py
+++ b/solution.py
@@ -21,6 +21,7 @@
 BLOCK = 40
 SHARE = 5
 TILES = 5
+PACK = 24
 
 
 def halves(table):
@@ -67,6 +68,43 @@
     return lax.dot_general(a, b, (((1,), (1,)), ((), ())), preferred_element_type=F32)
 
 
+def moves(count, base):
+    found, slot, used = [], 0, 0
+    for group in range(base, count):
+        lane = 0
+        while lane < LAT:
+            n = min(LAT - lane, LANES - LAT - used)
+            found.append((group, lane, n, slot, LAT + used))
+            lane, used = lane + n, used + n
+            if used == LANES - LAT:
+                slot, used = slot + 1, 0
+    return found
+
+
+def between(start, n):
+    lane = lax.broadcasted_iota(jnp.int32, (8, LANES), 1)
+    return (lane >= start) & (lane < start + n)
+
+
+def packed(value, base):
+    groups = [value[8 * g : 8 * g + 8] for g in range(value.shape[0] // 8)]
+    kept = groups[:base]
+    for group, lane, n, slot, to in moves(len(groups), base):
+        moved = pltpu.roll(groups[group], to - lane, 1)
+        kept[slot] = jnp.where(between(to, n), moved, kept[slot])
+    return jnp.concatenate(kept, axis=0)
+
+
+def unpacked(value, count):
+    base = value.shape[0] // 8
+    groups = [value[8 * g : 8 * g + 8] for g in range(base)]
+    groups += [jnp.zeros((8, LANES), F32)] * (count - base)
+    for group, lane, n, slot, to in moves(count, base):
+        moved = pltpu.roll(groups[slot], LANES + lane - to, 1)
+        groups[group] = jnp.where(between(lane, n), moved, groups[group])
+    return jnp.concatenate(groups, axis=0)
+
+
 def remote(src, dst, send, recv, device):
     return pltpu.make_async_remote_copy(
         src_ref=src,
@@ -90,9 +128,14 @@
     inv_low,
     out,
     ext,
+    hs_right,
+    hs_left,
+    hr_right,
+    hr_left,
     wbuf,
     win,
     adv,
+    sent,
     r1,
     s2,
     r2,
@@ -117,12 +160,13 @@
     gbuf,
     syn,
     s4,
+    s4p,
     r4,
     yc,
     s5,
     r5,
     o6,
-    local_sem,
+    r6,
     w_sem,
     leg_sem,
     tab_sem,
@@ -155,9 +199,6 @@
     z, core = band // 2, band % 2
     odd = x % 2 == 1
 
-    own = pltpu.make_async_copy(field, ext.at[:, :, pl.ds(64, 160), :], local_sem)
-    own.start()
-
     def w_copy(h, t):
         return pltpu.make_async_copy(weight.at[h, t], wbuf.at[h, t], w_sem.at[h, t])
 
@@ -189,23 +230,17 @@
     for k in range(1, 4):
         greet((((z + k) % 4) * 2 + core, sec))
     greet((z * 2 + 1 - core, sec))
+
+    for h in range(2):
+        for v in range(2):
+            ext[h, v, 64:224, 0:LAT] = field[h, v]
+            hs_right[h * 2 + v] = packed(ext[h, v, 160:224, :], 5)
+            hs_left[h * 2 + v] = packed(ext[h, v, 64:160, :], 8)
+
     pl.semaphore_wait(barrier, 19)
-
     right, left = (sec + 1) % 16, (sec + 15) % 16
-    to_right = remote(
-        field.at[:, :, pl.ds(96, 64), :],
-        ext.at[:, :, pl.ds(0, 64), :],
-        halo_s.at[0],
-        halo_r.at[0],
-        (band, right),
-    )
-    to_left = remote(
-        field.at[:, :, pl.ds(0, 96), :],
-        ext.at[:, :, pl.ds(224, 96), :],
-        halo_s.at[1],
-        halo_r.at[1],
-        (band, left),
-    )
+    to_right = remote(hs_right, hr_right, halo_s.at[0], halo_r.at[0], (band, right))
+    to_left = remote(hs_left, hr_left, halo_s.at[1], halo_r.at[1], (band, left))
     to_right.start()
     to_left.start()
     adv[...] = jnp.zeros_like(adv)
@@ -214,9 +249,12 @@
     def _():
         r2[1] = jnp.zeros_like(r2[1])
 
-    own.wait()
     to_right.wait_recv()
     to_left.wait_recv()
+    for h in range(2):
+        for v in range(2):
+            ext[h, v, 0:64, :] = unpacked(hr_right[h * 2 + v], 8)
+            ext[h, v, 224:320, :] = unpacked(hr_left[h * 2 + v], 12)
 
     @pl.loop(0, 8)
     def _(q):
@@ -226,13 +264,13 @@
     def e1(t, k):
         to = (y + k) % 4
         return remote(
-            adv.at[to, t], r1.at[y, t], e1_s.at[t, k], e1_r.at[t, y], (band, to * 4 + x)
+            sent.at[to, t], r1.at[y, t], e1_s.at[t, k], e1_r.at[t, y], (band, to * 4 + x)
         )
 
     def e1_arrives(t, k):
         source = (y + k) % 4
         remote(
-            adv.at[source, t],
+            sent.at[source, t],
             r1.at[source, t],
             e1_s.at[t, k],
             e1_r.at[t, source],
@@ -277,10 +315,11 @@
                 for v in range(2):
                     total[v] = total[v] + win[v, j : j + 1, :] * w
             for v in range(2):
-                adv[h * 2 + v, t, :, 0:LAT] = total[v]
+                adv[h * 2 + v, :, 0:LAT] = total[v]
+                sent[h * 2 + v, t] = packed(adv[h * 2 + v], 3)
         for k in range(1, 4):
             e1(t, k).start()
-        r1[y, t] = adv[y, t]
+        r1[y, t] = sent[y, t]
 
     def radix(t):
         for k in range(1, 4):
@@ -319,7 +358,7 @@
     def _(i):
         part, source = i // 4, i % 4
         for t in range(TILES):
-            high, low = split(r2[part, source, t])
+            high, low = split(unpacked(r2[part, source, t], 4))
             start = pl.multiple_of(i * 160 + t * TILE, TILE)
             zc[pl.ds(start, TILE), 0:LANES] = high
             zc[pl.ds(start, TILE), LANES : 2 * LANES] = low
@@ -338,7 +377,7 @@
         value = both[:, 0:LANES] + both[:, LANES:] + dot(fl[rows, :], zc[:, 0:LANES])
         for q in range(4):
             d = group * 4 + q
-            s3[d] = value[q * BLOCK : (q + 1) * BLOCK]
+            s3[d] = packed(value[q * BLOCK : (q + 1) * BLOCK], 4)
 
             @pl.when(d != sec)
             def _():
@@ -346,7 +385,7 @@
 
             @pl.when(d == sec)
             def _():
-                r3[d] = value[q * BLOCK : (q + 1) * BLOCK]
+                r3[d] = s3[d]
 
     loads[2].start()
     loads[3].start()
@@ -373,8 +412,8 @@
     for v in range(2):
         for c in range(4):
             north, south = r3[v * 4 + c], r3[8 + v * 4 + c]
-            eo[0, v, c] = north + south
-            eo[1, v, c] = north - south
+            eo[0, v, c] = unpacked(north + south, 5)
+            eo[1, v, c] = unpacked(north - south, 5)
     for p in range(BLOCK):
         j, c = p // 4, p % 4
         for s in range(2):
@@ -585,13 +624,15 @@
 
     def e4(k):
         to = (sec + k) % 16
-        return remote(s4.at[to], r4.at[sec], e4_s.at[k], e4_r.at[sec], (band, to))
+        return remote(s4p.at[to], r4.at[sec], e4_s.at[k], e4_r.at[sec], (band, to))
 
     @pl.loop(1, 16)
     def _(k):
+        to = (sec + k) % 16
+        s4p[to] = packed(s4[to], 4)
         e4(k).start()
 
-    r4[sec] = s4[sec]
+    r4[sec] = packed(s4[sec], 4)
     loads[2].wait()
     loads[3].wait()
 
@@ -599,55 +640,55 @@
     def _(k):
         source = (sec + k) % 16
         remote(
-            s4.at[source], r4.at[source], e4_s.at[k], e4_r.at[source], (band, source)
+            s4p.at[source], r4.at[source], e4_s.at[k], e4_r.at[source], (band, source)
         ).wait_recv()
 
     @pl.loop(0, 8)
     def _(i):
-        pair = jnp.concatenate([r4[2 * i], r4[2 * i + 1]], axis=0)
+        pair = jnp.concatenate([unpacked(r4[2 * i], 5), unpacked(r4[2 * i + 1], 5)], axis=0)
         high, low = split(pair)
         start = pl.multiple_of(i * 80, 80)
         yc[pl.ds(start, 80), 0:LANES] = high
         yc[pl.ds(start, 80), LANES : 2 * LANES] = low
 
-    def e5(k, part):
+    def e5(k, part, half):
         to = (x + k) % 4
         return remote(
-            s5.at[part, to],
-            r5.at[part, x],
-            e5_s.at[part, k],
-            e5_r.at[part, x],
+            s5.at[part, to, half],
+            r5.at[part, x, half],
+            e5_s.at[part, half, k],
+            e5_r.at[part, half, x],
             (band, y * 4 + to),
         )
 
-    def e5_arrives(k, part):
+    def e5_arrives(k, part, half):
         source = (x + k) % 4
         remote(
-            s5.at[part, source],
-            r5.at[part, source],
-            e5_s.at[part, k],
-            e5_r.at[part, source],
+            s5.at[part, source, half],
+            r5.at[part, source, half],
+            e5_s.at[part, half, k],
+            e5_r.at[part, half, source],
             (band, y * 4 + source),
         ).wait_recv()
 
-    @pl.loop(0, 4)
+    @pl.loop(0, 8)
     def _(g):
-        k = (g + 1) % 4
+        half, k = g // 4, (g + 1) % 4
         to = (x + k) % 4
 
         def part_of(part):
-            rows = pl.ds(pl.multiple_of((to * 2 + part) * 160, 160), 160)
+            rows = pl.ds(pl.multiple_of((to * 2 + part) * 160 + half * 80, 80), 80)
             both = dot(ih[rows, :], yc[...])
             value = both[:, 0:LANES] + both[:, LANES:] + dot(il[rows, :], yc[:, 0:LANES])
-            s5[part, to] = value
+            s5[part, to, half] = packed(value, 7)
 
             @pl.when(k != 0)
             def _():
-                e5(k, part).start()
+                e5(k, part, half).start()
 
             @pl.when(k == 0)
             def _():
-                r5[part, to] = value
+                r5[part, to, half] = s5[part, to, half]
 
         part_of(0)
 
@@ -655,44 +696,44 @@
         def _():
             part_of(1)
 
-    for k in range(1, 4):
-        e5_arrives(k, 0)
-
-        @pl.when((x + k) % 2 == 1)
-        def _():
-            e5_arrives(k, 1)
-
-    def e6(t, k):
+    def e6(half, k):
         to = (y + k) % 4
         return remote(
-            o6.at[to, t], out.at[y, t], e6_s.at[t, k], e6_r.at[t, y], (band, to * 4 + x)
+            o6.at[to, half], r6.at[y, half], e6_s.at[half, k], e6_r.at[half, y], (band, to * 4 + x)
         )
 
-    @pl.loop(0, TILES)
-    def _(t):
-        rows = pl.ds(pl.multiple_of(t * TILE, TILE), TILE)
-        a, c = r5[0, 0, rows, :], r5[0, 2, rows, :]
-        b = r5[0, 1, rows, :] + r5[0, 3, rows, :]
-        d = r5[1, 3, rows, :] - r5[1, 1, rows, :]
-        o6[0, t] = (a + c) + b
-        o6[1, t] = (a - c) + d
-        o6[2, t] = (a + c) - b
-        o6[3, t] = (a - c) - d
+    @pl.loop(0, 2)
+    def _(half):
         for k in range(1, 4):
-            e6(t, k).start()
-        out[y, t] = o6[y, t]
-
-    @pl.loop(0, TILES)
-    def _(t):
+            e5_arrives(k, 0, half)
+
+            @pl.when((x + k) % 2 == 1)
+            def _():
+                e5_arrives(k, 1, half)
+
+        a, c = r5[0, 0, half], r5[0, 2, half]
+        b = r5[0, 1, half] + r5[0, 3, half]
+        d = r5[1, 3, half] - r5[1, 1, half]
+        o6[0, half] = (a + c) + b
+        o6[1, half] = (a - c) + d
+        o6[2, half] = (a + c) - b
+        o6[3, half] = (a - c) - d
+        for k in range(1, 4):
+            e6(half, k).start()
+        out[y, half] = unpacked(o6[y, half], 10)
+
+    @pl.loop(0, 2)
+    def _(half):
         for k in range(1, 4):
             source = (y + k) % 4
             remote(
-                o6.at[source, t],
-                out.at[source, t],
-                e6_s.at[t, k],
-                e6_r.at[t, source],
+                o6.at[source, half],
+                r6.at[source, half],
+                e6_s.at[half, k],
+                e6_r.at[half, source],
                 (band, source * 4 + x),
             ).wait_recv()
+            out[source, half] = unpacked(r6[source, half], 10)
 
     to_right.wait_send()
     to_left.wait_send()
@@ -707,8 +748,6 @@
             def _():
                 e2(t, k, 1).wait_send()
 
-            e6(t, k).wait_send()
-
     @pl.loop(1, 16)
     def _(k):
         e3((sec + k) % 16).wait_send()
@@ -719,34 +758,41 @@
     for copy in (half_up, half_down, early_up, early_down, late_up, late_down, *sends):
         copy.wait_send()
     for k in range(1, 4):
-        e5(k, 0).wait_send()
-
-        @pl.when(odd)
-        def _():
-            e5(k, 1).wait_send()
+        for half in range(2):
+            e5(k, 0, half).wait_send()
+
+            @pl.when(odd)
+            def _():
+                e5(k, 1, half).wait_send()
+
+            e6(half, k).wait_send()
 
 
 def local(field, depart, interp_weight, legendre, damping):
-    moved = jnp.pad(jnp.transpose(field, (0, 2, 3, 1)), ((0, 0),) * 3 + ((0, LANES - LAT),))
     forward, inverse = tables()
     constants = [jnp.asarray(t) for t in (*halves(forward), *halves(inverse))]
     vmem = pl.BlockSpec(memory_space=pltpu.VMEM)
     hbm = pl.BlockSpec(memory_space=pl.ANY)
     scratch = [
         pltpu.VMEM((2, 2, 320, LANES), F32),
+        pltpu.VMEM((4, 40, LANES), F32),
+        pltpu.VMEM((4, 64, LANES), F32),
+        pltpu.VMEM((4, 40, LANES), F32),
+        pltpu.VMEM((4, 64, LANES), F32),
         pltpu.VMEM((2, 5, 64, TILE, LAT), BF16),
         pltpu.VMEM((2, 64, LAT), F32),
-        pltpu.VMEM((4, 5, TILE, LANES), F32),
-        pltpu.VMEM((4, 5, TILE, LANES), F32),
-        pltpu.VMEM((4, 5, TILE, LANES), F32),
-        pltpu.VMEM((2, 4, 5, TILE, LANES), F32),
+        pltpu.VMEM((4, TILE, LANES), F32),
+        pltpu.VMEM((4, 5, PACK, LANES), F32),
+        pltpu.VMEM((4, 5, PACK, LANES), F32),
+        pltpu.VMEM((4, 5, PACK, LANES), F32),
+        pltpu.VMEM((2, 4, 5, PACK, LANES), F32),
         pltpu.VMEM((1280, 2 * LANES), BF16),
         pltpu.VMEM((640, 1280), BF16),
         pltpu.VMEM((640, 1280), BF16),
         pltpu.VMEM((1280, 640), BF16),
         pltpu.VMEM((1280, 640), BF16),
-        pltpu.VMEM((16, BLOCK, LANES), F32),
-        pltpu.VMEM((16, BLOCK, LANES), F32),
+        pltpu.VMEM((16, 32, LANES), F32),
+        pltpu.VMEM((16, 32, LANES), F32),
         pltpu.VMEM((2, 2, 4, BLOCK, LANES), F32),
         pltpu.VMEM((BLOCK, 16, LANES), F32),
         pltpu.VMEM((BLOCK, 32, LANES), BF16),
@@ -761,15 +807,16 @@
         pltpu.VMEM((8, SHARE, 4, WIDE), F32),
         pltpu.VMEM((BLOCK, 16, LANES), F32),
         pltpu.VMEM((16, BLOCK, LANES), F32),
-        pltpu.VMEM((16, BLOCK, LANES), F32),
+        pltpu.VMEM((16, 32, LANES), F32),
+        pltpu.VMEM((16, 32, LANES), F32),
         pltpu.VMEM((640, 2 * LANES), BF16),
-        pltpu.VMEM((2, 4, 160, LANES), F32),
-        pltpu.VMEM((2, 4, 160, LANES), F32),
-        pltpu.VMEM((4, 5, TILE, LANES), F32),
+        pltpu.VMEM((2, 4, 2, 56, LANES), F32),
+        pltpu.VMEM((2, 4, 2, 56, LANES), F32),
+        pltpu.VMEM((4, 2, 56, LANES), F32),
+        pltpu.VMEM((4, 2, 56, LANES), F32),
     ]
     dma = pltpu.SemaphoreType.DMA
     scratch += [
-        dma,
         dma((2, 5)),
         dma((8,)),
         dma((4,)),
@@ -791,14 +838,14 @@
         dma((5,)),
         dma((16,)),
         dma((16,)),
+        dma((2, 2, 4)),
+        dma((2, 2, 4)),
         dma((2, 4)),
         dma((2, 4)),
-        dma((5, 4)),
-        dma((5, 4)),
     ]
     grid = pl.pallas_call(
         kernel,
-        out_shape=jax.ShapeDtypeStruct((4, 5, TILE, LANES), F32),
+        out_shape=jax.ShapeDtypeStruct((4, 2, 80, LANES), F32),
         in_specs=[vmem, vmem, hbm, hbm, pl.BlockSpec(memory_space=pltpu.SMEM)] + [hbm] * 4,
         out_specs=vmem,
         scratch_shapes=scratch,
@@ -806,7 +853,7 @@
             collective_id=0, has_side_effects=True, vmem_limit_bytes=62 * 1024 * 1024
         ),
     )(
-        moved,
+        jnp.transpose(field, (0, 2, 3, 1)),
         jnp.transpose(depart, (2, 0, 1)),
         jnp.transpose(interp_weight, (0, 2, 3, 4, 1)),
         legendre,

time: 82.2 us -> 79.2 us (0.964)
  Pallas kernels: 77.9 us -> 75.2 us
    pallas_call x1, Pallas kernels: 77.9 us -> 75.2 us  [local(): pl.pallas_call(kernel, out_shape=jax.ShapeDtypeStruct((4, 2, 80, LANES),...]
where the time goes in v3:
time: 79.2 us; the launch traced here: 79 us
  Pallas kernels  75.2 us (95%)
  local copies, waits for them, and re-layouts  3.76 us (5%)
    pallas_call x1, Pallas kernels, local(): pl.pallas_call(kernel, out_shape=jax.ShapeDtypeStruct((4, 2, 80, LANES),...  75.2 us
    unnamed x2, local copies, waits for them, and re-layouts  3.76 us

profile of v3, /device:TPU:0, one launch (start us, length us, event | category | flops | bytes accessed | tf_op | source)
XLA Modules:
  0.0 79.0 jit_solution(11384265936821904776)
XLA Ops:
  0.0 1.9 %copy.10 = f32[2,80,2,160]{1,3,2,0:T(8,128)} copy(f32[2,80,2,160]{3,2,1,0:T(2,128)} %param.9) | data formatting | bytes 409600 | tf_op args[0]
  1.9 75.2 %shard_map.91 = f32[4,2,80,128]{3,2,1,0:T(8,128)} custom-call(f32[2,2,160,80]{3,2,1,0:T(8,128)} %bitcast.8, s32[5,2,80]{2,1,0:T(2,128)} %bitcast.9, bf16[2,5,64,32,80]{4,3,2,1,0:T(8,128)(2,1)} %bitcast.6, f32[40,80,1281]{2,1,0:T(8,128)} %legendre.1, f32[2]{0:T(128)} %damping.1, bf16[4,640,1280]{2,1,0:T(8,128)(2,1)} %constant.8.clone.fwd_high, ...), custom_call_target="tpu_custom_call" | custom-call | tf_op jit(solution)/shard_map/pallas_call | solution.py:846
  77.1 1.9 %copy.12 = f32[2,2,160,80]{2,1,3,0:T(2,128)} copy(f32[2,2,160,80]{3,2,1,0:T(8,128)} %bitcast.7) | data formatting | bytes 409600

commit v4 on v3

--- a/solution.py
+++ b/solution.py
@@ -128,10 +128,8 @@
     inv_low,
     out,
     ext,
-    hs_right,
-    hs_left,
-    hr_right,
-    hr_left,
+    hs,
+    hr,
     wbuf,
     win,
     adv,
@@ -234,27 +232,22 @@
     for h in range(2):
         for v in range(2):
             ext[h, v, 64:224, 0:LAT] = field[h, v]
-            hs_right[h * 2 + v] = packed(ext[h, v, 160:224, :], 5)
-            hs_left[h * 2 + v] = packed(ext[h, v, 64:160, :], 8)
+            for i, start in enumerate((64, 192, 96, 160, 128)):
+                hs[i, h * 2 + v] = packed(ext[h, v, start : start + TILE, :], 3)
 
     pl.semaphore_wait(barrier, 19)
-    right, left = (sec + 1) % 16, (sec + 15) % 16
-    to_right = remote(hs_right, hr_right, halo_s.at[0], halo_r.at[0], (band, right))
-    to_left = remote(hs_left, hr_left, halo_s.at[1], halo_r.at[1], (band, left))
-    to_right.start()
-    to_left.start()
+
+    def halo(i):
+        to = (sec + 15 - 14 * (i % 2)) % 16
+        return remote(hs.at[i], hr.at[i], halo_s.at[i], halo_r.at[i], (band, to))
+
+    for i in range(TILES):
+        halo(i).start()
     adv[...] = jnp.zeros_like(adv)
 
     @pl.when(jnp.logical_not(odd))
     def _():
         r2[1] = jnp.zeros_like(r2[1])
-
-    to_right.wait_recv()
-    to_left.wait_recv()
-    for h in range(2):
-        for v in range(2):
-            ext[h, v, 0:64, :] = unpacked(hr_right[h * 2 + v], 8)
-            ext[h, v, 224:320, :] = unpacked(hr_left[h * 2 + v], 12)
 
     @pl.loop(0, 8)
     def _(q):
@@ -298,7 +291,17 @@
             (band, y * 4 + source),
         ).wait_recv()
 
-    def advect(t):
+    def tile_of(i):
+        return 2 + (1 - 2 * (i % 2)) * ((i + 1) // 2)
+
+    def advect(i):
+        t = tile_of(i)
+        halo(i).wait_recv()
+        start = (1 - i % 2) * (224 + 16 * i) + (i % 2) * (48 - 16 * i)
+        rows = pl.ds(pl.multiple_of(start, TILE), TILE)
+        for h in range(2):
+            for v in range(2):
+                ext[h, v, rows, :] = unpacked(hr[i, h * 2 + v], 4)
         for h in range(2):
             w_copy(h, t).wait()
             dep = depart[t, h : h + 1, :]
@@ -321,7 +324,8 @@
             e1(t, k).start()
         r1[y, t] = sent[y, t]
 
-    def radix(t):
+    def radix(i):
+        t = tile_of(i)
         for k in range(1, 4):
             e1_arrives(t, k)
         a, b, c, d = r1[0, t], r1[1, t], r1[2, t], r1[3, t]
@@ -458,12 +462,6 @@
     def share_at(k, which):
         return ((z + 2 + 3 * k + 3 * (k // 2) + 2 * (k // 3)) % 4) * 2 + which
 
-    @pl.loop(0, 4)
-    def _(k):
-        for i, value in enumerate(analyse(share_at(k, 1 - core))):
-            pbuf[k, i, :, 0:ROWS] = value
-        c1(k).start()
-
     first, last = pl.ds(0, 3), pl.ds(3, 2)
     half_up = remote(sbuf.at[0, first], rbuf.at[first], c2_s.at[0], c2_r.at[0], up)
     half_down = remote(sbuf.at[0, last], rbuf.at[last], c2_s.at[1], c2_r.at[1], down)
@@ -472,27 +470,42 @@
     late_up = remote(sbuf.at[1, first], tbuf.at[0, first], c2_s.at[4], c2_r.at[4], up)
     late_down = remote(sbuf.at[2, last], tbuf.at[1, last], c2_s.at[5], c2_r.at[5], down)
 
-    @pl.loop(0, 4)
-    def _(k):
-        values = analyse(share_at(k, core))
-        for i, value in enumerate(values):
-            sbuf[k, i, :, 0:ROWS] = value
-        c1(k).wait_recv()
-        for i in range(SHARE):
-            sbuf[k, i] = sbuf[k, i] + cbuf[k, i]
-
-        @pl.when(k == 0)
+    @pl.loop(0, 8)
+    def _(n):
+        late = n // 4
+        mine = (1 - late) * (n // 2) + late * (n % 2)
+        k = (1 - late) * (n % 2) + late * (n // 2)
+        values = analyse(share_at(k, core + (1 - mine) * (1 - 2 * core)))
+
+        @pl.when(mine == 0)
+        def _():
+            for i, value in enumerate(values):
+                pbuf[k, i, :, 0:ROWS] = value
+            c1(k).start()
+
+        @pl.when(mine == 1)
+        def _():
+            for i, value in enumerate(values):
+                sbuf[k, i, :, 0:ROWS] = value
+            c1(k).wait_recv()
+            for i in range(SHARE):
+                sbuf[k, i] = sbuf[k, i] + cbuf[k, i]
+
+        @pl.when(n == 2)
         def _():
             half_up.start()
             half_down.start()
 
-        @pl.when(k == 1)
+        @pl.when(n == 3)
         def _():
             early_up.start()
 
-        @pl.when(k == 2)
+        @pl.when(n == 5)
         def _():
             early_down.start()
+
+        @pl.when(n == 6)
+        def _():
             half_up.wait_recv()
             for i in range(3):
                 sbuf[1, i] = sbuf[1, i] + rbuf[i]
@@ -735,8 +748,8 @@
             ).wait_recv()
             out[source, half] = unpacked(r6[source, half], 10)
 
-    to_right.wait_send()
-    to_left.wait_send()
+    for i in range(TILES):
+        halo(i).wait_send()
 
     @pl.loop(0, TILES)
     def _(t):
@@ -775,10 +788,8 @@
     hbm = pl.BlockSpec(memory_space=pl.ANY)
     scratch = [
         pltpu.VMEM((2, 2, 320, LANES), F32),
-        pltpu.VMEM((4, 40, LANES), F32),
-        pltpu.VMEM((4, 64, LANES), F32),
-        pltpu.VMEM((4, 40, LANES), F32),
-        pltpu.VMEM((4, 64, LANES), F32),
+        pltpu.VMEM((5, 4, PACK, LANES), F32),
+        pltpu.VMEM((5, 4, PACK, LANES), F32),
         pltpu.VMEM((2, 5, 64, TILE, LAT), BF16),
         pltpu.VMEM((2, 64, LAT), F32),
         pltpu.VMEM((4, TILE, LANES), F32),
@@ -820,8 +831,8 @@
         dma((2, 5)),
         dma((8,)),
         dma((4,)),
-        dma((2,)),
-        dma((2,)),
+        dma((5,)),
+        dma((5,)),
         dma((5, 4)),
         dma((5, 4)),
         dma((2, 5, 4)),

time: 79.2 us -> 77.7 us (0.981)
  Pallas kernels: 75.2 us -> 73.8 us
    pallas_call x1, Pallas kernels: 75.2 us -> 73.8 us  [local(): pl.pallas_call(kernel, out_shape=jax.ShapeDtypeStruct((4, 2, 80, LANES),...]
where the time goes in v4:
time: 77.7 us; the launch traced here: 77.6 us
  Pallas kernels  73.8 us (95%)
  local copies, waits for them, and re-layouts  3.76 us (5%)
    pallas_call x1, Pallas kernels, local(): pl.pallas_call(kernel, out_shape=jax.ShapeDtypeStruct((4, 2, 80, LANES),...  73.8 us
    unnamed x2, local copies, waits for them, and re-layouts  3.76 us

profile of v4, /device:TPU:0, one launch (start us, length us, event | category | flops | bytes accessed | tf_op | source)
XLA Modules:
  0.0 77.6 jit_solution(2424453620354261062)
XLA Ops:
  0.0 1.9 %copy.10 = f32[2,80,2,160]{1,3,2,0:T(8,128)} copy(f32[2,80,2,160]{3,2,1,0:T(2,128)} %param.9) | data formatting | bytes 409600 | tf_op args[0]
  1.9 73.8 %shard_map.91 = f32[4,2,80,128]{3,2,1,0:T(8,128)} custom-call(f32[2,2,160,80]{3,2,1,0:T(8,128)} %bitcast.8, s32[5,2,80]{2,1,0:T(2,128)} %bitcast.9, bf16[2,5,64,32,80]{4,3,2,1,0:T(8,128)(2,1)} %bitcast.6, f32[40,80,1281]{2,1,0:T(8,128)} %legendre.1, f32[2]{0:T(128)} %damping.1, bf16[4,640,1280]{2,1,0:T(8,128)(2,1)} %constant.8.clone.fwd_high, ...), custom_call_target="tpu_custom_call" | custom-call | tf_op jit(solution)/shard_map/pallas_call | solution.py:857
  75.7 1.9 %copy.12 = f32[2,2,160,80]{2,1,3,0:T(2,128)} copy(f32[2,2,160,80]{3,2,1,0:T(8,128)} %bitcast.7) | data formatting | bytes 409600

commit v5 on v4

--- a/solution.py
+++ b/solution.py
@@ -49,7 +49,7 @@
     real = np.stack([cos, -sin], axis=4).reshape(4, 640, 640)
     imag = np.stack([sin, cos], axis=4).reshape(4, 640, 640)
     both = np.stack([real, imag], axis=1)
-    both = both.reshape(4, 2, 640, 4, 160).transpose(0, 3, 1, 4, 2)
+    both = both.reshape(4, 2, 640, 4, 2, 80).transpose(0, 4, 1, 3, 5, 2)
     inverse = both.reshape(4, 1280, 640)
     return forward, inverse
 
@@ -350,7 +350,8 @@
     pl.loop(0, TILES)(radix)
 
     @pl.loop(0, TILES)
-    def _(t):
+    def _(i):
+        t = tile_of(i)
         for k in range(1, 4):
             e2_arrives(t, k, 0)
 
@@ -358,14 +359,12 @@
             def _():
                 e2_arrives(t, k, 1)
 
-    @pl.loop(0, 8)
-    def _(i):
-        part, source = i // 4, i % 4
-        for t in range(TILES):
-            high, low = split(unpacked(r2[part, source, t], 4))
-            start = pl.multiple_of(i * 160 + t * TILE, TILE)
-            zc[pl.ds(start, TILE), 0:LANES] = high
-            zc[pl.ds(start, TILE), LANES : 2 * LANES] = low
+        for part in range(2):
+            for source in range(4):
+                high, low = split(unpacked(r2[part, source, t], 4))
+                start = pl.multiple_of((part * 4 + source) * 160 + t * TILE, TILE)
+                zc[pl.ds(start, TILE), 0:LANES] = high
+                zc[pl.ds(start, TILE), LANES : 2 * LANES] = low
 
     loads[0].wait()
     loads[1].wait()
@@ -373,14 +372,14 @@
     def e3(d):
         return remote(s3.at[d], r3.at[sec], e3_s.at[d], e3_r.at[sec], (band, d))
 
-    @pl.loop(0, 4)
+    @pl.loop(0, 2)
     def _(g):
-        group = (g + sec // 4) % 4
-        rows = pl.ds(pl.multiple_of(group * 160, 160), 160)
+        group = (g + sec // 8) % 2
+        rows = pl.ds(pl.multiple_of(group * 320, 320), 320)
         both = dot(fh[rows, :], zc[...])
         value = both[:, 0:LANES] + both[:, LANES:] + dot(fl[rows, :], zc[:, 0:LANES])
-        for q in range(4):
-            d = group * 4 + q
+        for q in range(8):
+            d = group * 8 + q
             s3[d] = packed(value[q * BLOCK : (q + 1) * BLOCK], 4)
 
             @pl.when(d != sec)
@@ -649,15 +648,17 @@
     loads[2].wait()
     loads[3].wait()
 
-    @pl.loop(1, 16)
-    def _(k):
-        source = (sec + k) % 16
-        remote(
-            s4p.at[source], r4.at[source], e4_s.at[k], e4_r.at[source], (band, source)
-        ).wait_recv()
-
     @pl.loop(0, 8)
-    def _(i):
+    def _(n):
+        i = (sec // 2 + n) % 8
+        for source in (2 * i, 2 * i + 1):
+
+            @pl.when(source != sec)
+            def _():
+                remote(
+                    s4p.at[source], r4.at[source], e4_s.at[0], e4_r.at[source], (band, source)
+                ).wait_recv()
+
         pair = jnp.concatenate([unpacked(r4[2 * i], 5), unpacked(r4[2 * i + 1], 5)], axis=0)
         high, low = split(pair)
         start = pl.multiple_of(i * 80, 80)
@@ -684,24 +685,22 @@
             (band, y * 4 + source),
         ).wait_recv()
 
-    @pl.loop(0, 8)
-    def _(g):
-        half, k = g // 4, (g + 1) % 4
-        to = (x + k) % 4
-
+    @pl.loop(0, 2)
+    def _(half):
         def part_of(part):
-            rows = pl.ds(pl.multiple_of((to * 2 + part) * 160 + half * 80, 80), 80)
+            rows = pl.ds(pl.multiple_of(half * 640 + part * 320, 320), 320)
             both = dot(ih[rows, :], yc[...])
             value = both[:, 0:LANES] + both[:, LANES:] + dot(il[rows, :], yc[:, 0:LANES])
-            s5[part, to, half] = packed(value, 7)
-
-            @pl.when(k != 0)
-            def _():
-                e5(k, part, half).start()
-
-            @pl.when(k == 0)
-            def _():
-                r5[part, to, half] = s5[part, to, half]
+            for to in range(4):
+                s5[part, to, half] = packed(value[to * 80 : (to + 1) * 80], 7)
+
+                @pl.when(to != x)
+                def _():
+                    e5((to - x + 4) % 4, part, half).start()
+
+                @pl.when(to == x)
+                def _():
+                    r5[part, to, half] = s5[part, to, half]
 
         part_of(0)
 

time: 77.7 us -> 76.3 us (0.982)
  Pallas kernels: 73.8 us -> 72.3 us
    pallas_call x1, Pallas kernels: 73.8 us -> 72.3 us  [local(): pl.pallas_call(kernel, out_shape=jax.ShapeDtypeStruct((4, 2, 80, LANES),...]
where the time goes in v5:
time: 76.3 us; the launch traced here: 76.1 us
  Pallas kernels  72.3 us (95%)
  local copies, waits for them, and re-layouts  3.76 us (5%)
    pallas_call x1, Pallas kernels, local(): pl.pallas_call(kernel, out_shape=jax.ShapeDtypeStruct((4, 2, 80, LANES),...  72.3 us
    unnamed x2, local copies, waits for them, and re-layouts  3.76 us

profile of v5, /device:TPU:0, one launch (start us, length us, event | category | flops | bytes accessed | tf_op | source)
XLA Modules:
  0.0 76.1 jit_solution(16080602043132693685)
XLA Ops:
  0.0 1.9 %copy.10 = f32[2,80,2,160]{1,3,2,0:T(8,128)} copy(f32[2,80,2,160]{3,2,1,0:T(2,128)} %param.9) | data formatting | bytes 409600 | tf_op args[0]
  1.9 72.3 %shard_map.91 = f32[4,2,80,128]{3,2,1,0:T(8,128)} custom-call(f32[2,2,160,80]{3,2,1,0:T(8,128)} %bitcast.8, s32[5,2,80]{2,1,0:T(2,128)} %bitcast.9, bf16[2,5,64,32,80]{4,3,2,1,0:T(8,128)(2,1)} %bitcast.6, f32[40,80,1281]{2,1,0:T(8,128)} %legendre.1, f32[2]{0:T(128)} %damping.1, bf16[4,640,1280]{2,1,0:T(8,128)(2,1)} %constant.8.clone.fwd_high, ...), custom_call_target="tpu_custom_call" | custom-call | tf_op jit(solution)/shard_map/pallas_call | solution.py:856
  74.2 1.9 %copy.12 = f32[2,2,160,80]{2,1,3,0:T(2,128)} copy(f32[2,2,160,80]{3,2,1,0:T(8,128)} %bitcast.7) | data formatting | bytes 409600

commit v6 on v5

--- a/solution.py
+++ b/solution.py
@@ -732,7 +732,7 @@
         o6[3, half] = (a - c) - d
         for k in range(1, 4):
             e6(half, k).start()
-        out[y, half] = unpacked(o6[y, half], 10)
+        r6[y, half] = o6[y, half]
 
     @pl.loop(0, 2)
     def _(half):
@@ -745,7 +745,10 @@
                 e6_r.at[half, source],
                 (band, source * 4 + x),
             ).wait_recv()
-            out[source, half] = unpacked(r6[source, half], 10)
+
+    for block in range(4):
+        rows = [unpacked(r6[block, half], 10) for half in range(2)]
+        out[block] = jnp.transpose(jnp.concatenate(rows, axis=0))[0:LAT]
 
     for i in range(TILES):
         halo(i).wait_send()
@@ -855,7 +858,7 @@
     ]
     grid = pl.pallas_call(
         kernel,
-        out_shape=jax.ShapeDtypeStruct((4, 2, 80, LANES), F32),
+        out_shape=jax.ShapeDtypeStruct((4, LAT, 160), F32),
         in_specs=[vmem, vmem, hbm, hbm, pl.BlockSpec(memory_space=pltpu.SMEM)] + [hbm] * 4,
         out_specs=vmem,
         scratch_shapes=scratch,
@@ -870,8 +873,7 @@
         damping,
         *constants,
     )
-    grid = grid.reshape(2, 2, 160, LANES)[..., 0:LAT]
-    return jnp.transpose(grid, (0, 3, 1, 2))
+    return jnp.transpose(grid.reshape(2, 2, LAT, 160), (0, 2, 1, 3))
 
 
 def solution(mesh):

time: 76.3 us -> 76.5 us (level)
    reshape x0 -> x1, local copies, waits for them, and re-layouts: none -> 1.95 us  [local(): return jnp.transpose(grid.reshape(2, 2, LAT, 160), (0, 2, 1, 3))]
    unnamed x2 -> x1, local copies, waits for them, and re-layouts: 3.76 us -> 1.87 us
where the time goes in v6:
time: 76.5 us; the launch traced here: 76.4 us
  Pallas kernels  72.5 us (95%)
  local copies, waits for them, and re-layouts  3.83 us (5%)
    pallas_call x1, Pallas kernels, local(): pl.pallas_call(kernel, out_shape=jax.ShapeDtypeStruct((4, LAT, 160), F32)...  72.5 us
    reshape x1, local copies, waits for them, and re-layouts, local(): return jnp.transpose(grid.reshape(2, 2, LAT, 160), (0, 2, 1, 3))  1.95 us
    unnamed x1, local copies, waits for them, and re-layouts  1.87 us

profile of v6, /device:TPU:0, one launch (start us, length us, event | category | flops | bytes accessed | tf_op | source)
XLA Modules:
  0.0 76.4 jit_solution(17169666381450709054)
XLA Ops:
  0.0 1.9 %copy.10 = f32[2,80,2,160]{1,3,2,0:T(8,128)} copy(f32[2,80,2,160]{3,2,1,0:T(2,128)} %param.9) | data formatting | bytes 409600 | tf_op args[0]
  1.9 72.5 %shard_map.91 = f32[4,80,160]{2,1,0:T(8,128)} custom-call(f32[2,2,160,80]{3,2,1,0:T(8,128)} %bitcast.9, s32[5,2,80]{2,1,0:T(2,128)} %bitcast.10, bf16[2,5,64,32,80]{4,3,2,1,0:T(8,128)(2,1)} %bitcast.7, f32[40,80,1281]{2,1,0:T(8,128)} %legendre.1, f32[2]{0:T(128)} %damping.1, bf16[4,640,1280]{2,1,0:T(8,128)(2,1)} %constant.8.clone.fwd_high, ...), custom_call_target="tpu_custom_call" | custom-call | tf_op jit(solution)/shard_map/pallas_call | solution.py:859
  74.4 2.0 %copy.13 = f32[2,2,80,160]{3,1,2,0:T(2,128)} copy(f32[2,2,80,160]{3,2,1,0:T(8,128)} %bitcast.8) | data formatting | bytes 409600 | tf_op jit(solution)/shard_map/reshape | solution.py:876

commit v7 on v5

--- a/solution.py
+++ b/solution.py
@@ -600,9 +600,13 @@
             for n in (0, 1):
                 arrivals[n].wait_recv()
                 sends[n + 2].start()
-            for n in (4, 5):
-                arrivals[n].wait_recv()
-                sends[n + 3].start()
+            arrivals[4].wait_recv()
+            sends[7].start()
+
+        @pl.when(k == 3)
+        def _():
+            arrivals[5].wait_recv()
+            sends[8].start()
 
         @pl.when(k == 4)
         def _():

time: 76.3 us -> 76.3 us (level)
  no operation moved by 1% of the time
where the time goes in v7:
time: 76.3 us; the launch traced here: 76.1 us
  Pallas kernels  72.3 us (95%)
  local copies, waits for them, and re-layouts  3.76 us (5%)
    pallas_call x1, Pallas kernels, local(): pl.pallas_call(kernel, out_shape=jax.ShapeDtypeStruct((4, 2, 80, LANES),...  72.3 us
    unnamed x2, local copies, waits for them, and re-layouts  3.76 us

profile of v7, /device:TPU:0, one launch (start us, length us, event | category | flops | bytes accessed | tf_op | source)
XLA Modules:
  0.0 76.1 jit_solution(968943804212089988)
XLA Ops:
  0.0 1.9 %copy.10 = f32[2,80,2,160]{1,3,2,0:T(8,128)} copy(f32[2,80,2,160]{3,2,1,0:T(2,128)} %param.9) | data formatting | bytes 409600 | tf_op args[0]
  1.9 72.3 %shard_map.91 = f32[4,2,80,128]{3,2,1,0:T(8,128)} custom-call(f32[2,2,160,80]{3,2,1,0:T(8,128)} %bitcast.8, s32[5,2,80]{2,1,0:T(2,128)} %bitcast.9, bf16[2,5,64,32,80]{4,3,2,1,0:T(8,128)(2,1)} %bitcast.6, f32[40,80,1281]{2,1,0:T(8,128)} %legendre.1, f32[2]{0:T(128)} %damping.1, bf16[4,640,1280]{2,1,0:T(8,128)(2,1)} %constant.8.clone.fwd_high, ...), custom_call_target="tpu_custom_call" | custom-call | tf_op jit(solution)/shard_map/pallas_call | solution.py:860
  74.2 1.9 %copy.12 = f32[2,2,160,80]{2,1,3,0:T(2,128)} copy(f32[2,2,160,80]{3,2,1,0:T(8,128)} %bitcast.7) | data formatting | bytes 409600
